TPU v7x, 32 devices: a whole 2x2x4 slice. The times are simulated.
32 devices in a mesh: feat: 4 (over x, core), rows: 8 (over z, y).
Axes of the slice: x: 2, y: 2, z: 4, core: 2. Of those that a mesh axis runs over, the one named last changes fastest.
Arguments:
- features: bfloat16 [16, 2, 1024, 100], P('rows', None, None, 'feat'), may hold values from -6 to 6
- feature_masks: int32 [16, 100], P(None, 'feat'), may hold values from 0 to 1, as said below
- table_map: int32 [16], P('rows'), may hold values from 0 to 15, each once
- owners: int32 [24], replicated, may hold values from 0 to 7, as said below
- out_grad: bfloat16 [16, 2, 1024, 512], P('rows', None, 'feat'), may hold values from -6 to 6
- weight_slots: float32 [32, 256, 512], P('rows')
- moment1_slots: float32 [32, 256, 512], P('rows')
- moment2_slots: float32 [32, 256, 512], P('rows')
- emb_weight: float32 [100, 512], P('feat'), may hold values from -0.625 to 0.625
- emb_moment1: float32 [100, 512], P('feat')
- emb_moment2: float32 [100, 512], P('feat')
- small_weight: float32 [10, 512], replicated
- small_moment1: float32 [10, 512], replicated
- small_moment2: float32 [10, 512], replicated
Outputs:
- layer_out: bfloat16 [16, 2, 1024, 512], P('rows', None, 'feat')
- grad_inputs: bfloat16 [16, 2, 1024, 100], P('rows', None, None, 'feat')
- grad_slots: float32 [32, 256, 512], P('rows')
- moment1_out: float32 [32, 256, 512], P('rows')
- moment2_out: float32 [32, 256, 512], P('rows')
- weight_out: float32 [32, 256, 512], P('rows')
- weight_copies: bfloat16 [32, 256, 512], P('rows')
- emb_grad: float32 [100, 512], P('feat')
- emb_moment1_out: float32 [100, 512], P('feat')
- emb_moment2_out: float32 [100, 512], P('feat')
- emb_weight_out: float32 [100, 512], P('feat')
- emb_copy: bfloat16 [100, 512], P('feat')
- small_grad: float32 [10, 512], replicated
- small_moment1_out: float32 [10, 512], replicated
- small_moment2_out: float32 [10, 512], replicated
- small_weight_out: float32 [10, 512], replicated
Inputs may be any that keep to these rules, and one draw needn't show every extreme that they name: `feature_masks`: each row is 1 on the first k features and 0 on the rest, k from 2 to 100; some table has all 100. `table_map`: A permutation of the table numbers. `owners`: no index owns more than 4 blocks, and some own exactly 4.
All inputs are finite; a program needn't handle non-finite values.
Results may differ from a plain program's by a relative error of at most 0.015.
Values may be sent and summed in bfloat16 or wider, within the bound.
A program may use at most 192 MiB of HBM per device.

v0:
```python
import jax
import jax.numpy as jnp
from jax import lax
from jax.sharding import PartitionSpec as P

HEADS = 4
HEAD_DIM = 128
STEP = 10


HIGH = lax.Precision.HIGHEST
LN_EPS = 1e-05
BETA_FIRST = 0.9
BETA_SECOND = 0.999
ADAM_EPS = 1e-08
DECAY = 0.01
RATE_MATRIX = 0.1
RATE_EMBED = 0.3
RATE_SMALL = 0.6


def layer_norm(values, gain, shift):
    center = values - jnp.mean(values, axis=-1, keepdims=True)
    spread = jnp.mean(center * center, axis=-1, keepdims=True)
    return center * lax.rsqrt(spread + LN_EPS) * gain + shift


def exact_gelu(values):
    return jax.nn.gelu(values, approximate=False)


def adamw(weight, grad, first, second, rate):
    first_new = BETA_FIRST * first + (1.0 - BETA_FIRST) * grad
    second_new = BETA_SECOND * second + (1.0 - BETA_SECOND) * grad * grad
    first_hat = first_new / (1.0 - BETA_FIRST**STEP)
    second_hat = second_new / (1.0 - BETA_SECOND**STEP)
    weight_new = weight - rate * (first_hat / (jnp.sqrt(second_hat) + ADAM_EPS) + DECAY * weight)
    return (first_new, second_new, weight_new)


def split_heads(matrix):
    return matrix.reshape(matrix.shape[0], HEADS, HEAD_DIM)


def attend_forward(operands):
    query, keys, values = operands
    scale = HEAD_DIM ** (-0.5)
    scores = (
        jnp.einsum(
            "qhd,khd->hqk",
            split_heads(query),
            split_heads(keys),
            preferred_element_type=jnp.float32,
        )
        * scale
    )
    highest = jnp.max(scores, axis=-1, keepdims=True)
    weights = jnp.exp(scores - highest)
    totals = jnp.sum(weights, axis=-1, keepdims=True)
    probs = (weights / totals).astype(jnp.bfloat16)
    mixed = jnp.einsum(
        "hqk,khd->qhd", probs, split_heads(values), preferred_element_type=jnp.float32
    )
    return (
        mixed.reshape(query.shape[0], -1).astype(jnp.bfloat16),
        (highest + jnp.log(totals))[..., 0],
    )


def attend_backward(operands):
    query, keys, values, grad_mixed, log_totals = operands
    scale = HEAD_DIM ** (-0.5)
    q_heads = split_heads(query)
    k_heads = split_heads(keys)
    g_heads = split_heads(grad_mixed)
    scores = (
        jnp.einsum("qhd,khd->hqk", q_heads, k_heads, preferred_element_type=jnp.float32) * scale
    )
    probs = jnp.exp(scores - log_totals[..., None])
    grad_probs = jnp.einsum(
        "qhd,khd->hqk", g_heads, split_heads(values), preferred_element_type=jnp.float32
    )
    inner = jnp.sum(probs * grad_probs, axis=-1, keepdims=True)
    grad_scores = (probs * (grad_probs - inner)).astype(jnp.bfloat16)
    grad_query = (
        jnp.einsum("hqk,khd->qhd", grad_scores, k_heads, preferred_element_type=jnp.float32) * scale
    )
    grad_keys = (
        jnp.einsum("hqk,qhd->khd", grad_scores, q_heads, preferred_element_type=jnp.float32) * scale
    )
    grad_values = jnp.einsum(
        "hqk,qhd->khd", probs.astype(jnp.bfloat16), g_heads, preferred_element_type=jnp.float32
    )
    return (
        grad_query.reshape(query.shape[0], -1).astype(jnp.bfloat16),
        grad_keys.reshape(keys.shape[0], -1),
        grad_values.reshape(keys.shape[0], -1),
    )


def body(
    features,
    feature_masks,
    table_map,
    owners,
    out_grad,
    weight_slots,
    moment1_slots,
    moment2_slots,
    emb_weight,
    emb_moment1,
    emb_moment2,
    small_weight,
    small_moment1,
    small_moment2,
):
    unit_count = owners.shape[0]
    capacity = weight_slots.shape[0]
    block_rows = weight_slots.shape[1]
    width = weight_slots.shape[2]
    my_row = lax.axis_index("rows")
    same_owner = owners[:, None] == owners[None, :]
    earlier = lax.broadcasted_iota(jnp.int32, (unit_count, unit_count), 1) < lax.broadcasted_iota(
        jnp.int32, (unit_count, unit_count), 0
    )
    owner_rank = jnp.sum((same_owner & earlier).astype(jnp.int32), axis=1)
    slot_iota = lax.broadcasted_iota(jnp.int32, (capacity, unit_count), 0)
    selector = ((owners[None, :] == my_row) & (owner_rank[None, :] == slot_iota)).astype(
        jnp.float32
    )
    slot_ids = owners * capacity + owner_rank
    piece = lax.all_gather(weight_slots.astype(jnp.bfloat16), "rows", axis=0, tiled=True)
    count = piece.shape[0]
    piece_iota = lax.broadcasted_iota(jnp.int32, (unit_count, count), 1)
    picks = (slot_ids[:, None] == piece_iota).astype(jnp.bfloat16)
    gathered = jnp.einsum("ic,cxy->ixy", picks, piece, preferred_element_type=jnp.float32)
    matrices = gathered.reshape(-1, width, width).astype(jnp.bfloat16)
    w_query = matrices[0]
    w_key = matrices[1]
    w_value = matrices[2]
    w_out = matrices[3]
    w_up = matrices[4:8].transpose(1, 0, 2).reshape(width, 4 * width)
    w_down = matrices[8:12].reshape(4 * width, width)
    local_tables = features.shape[0]
    table_iota = lax.broadcasted_iota(jnp.int32, (local_tables, feature_masks.shape[0]), 1)
    picker = (table_map[:, None] == table_iota).astype(jnp.float32)
    mask_local = jnp.dot(picker, feature_masks.astype(jnp.float32), precision=HIGH)
    masked = features * mask_local[:, None, None, :].astype(jnp.bfloat16)
    emb_low = emb_weight.astype(jnp.bfloat16)
    rows_features = lax.all_to_all(masked, "feat", split_axis=2, concat_axis=3, tiled=True)
    emb_whole = lax.all_gather(emb_low, "feat", axis=0, tiled=True)
    hidden0 = (
        jnp.einsum("tshf,fd->tshd", rows_features, emb_whole, preferred_element_type=jnp.float32)
        + small_weight[0]
    )
    row_shape = hidden0.shape
    quarter_rows = row_shape[2]
    rows_total = row_shape[0] * row_shape[1] * row_shape[2]
    flat0 = hidden0.reshape(rows_total, width)
    normed1, norm1_pull = jax.vjp(layer_norm, flat0, small_weight[1], small_weight[2])
    act1 = normed1.astype(jnp.bfloat16)
    query = jnp.dot(act1, w_query, preferred_element_type=jnp.float32).astype(jnp.bfloat16)
    support = act1.reshape(local_tables, 2, quarter_rows, width)[:, 0]
    keys_local = jnp.einsum(
        "tjd,de->tje", support, w_key, preferred_element_type=jnp.float32
    ).astype(jnp.bfloat16)
    values_local = jnp.einsum(
        "tjd,de->tje", support, w_value, preferred_element_type=jnp.float32
    ).astype(jnp.bfloat16)
    keys_all, values_all = (
        lax.all_gather(keys_local, "feat", axis=1, tiled=True),
        lax.all_gather(values_local, "feat", axis=1, tiled=True),
    )
    query_tables = query.reshape(local_tables, 2 * quarter_rows, width)
    mixed, log_totals = lax.map(attend_forward, (query_tables, keys_all, values_all))
    mixed_flat = mixed.reshape(rows_total, width)
    resid1 = flat0 + jnp.dot(mixed_flat, w_out, preferred_element_type=jnp.float32)
    normed2, norm2_pull = jax.vjp(layer_norm, resid1, small_weight[3], small_weight[4])
    act2 = normed2.astype(jnp.bfloat16)
    pre_gelu = jnp.dot(act2, w_up, preferred_element_type=jnp.float32) + small_weight[6:10].reshape(
        4 * width
    )
    gelu_out, gelu_pull = jax.vjp(exact_gelu, pre_gelu)
    gelu_low = gelu_out.astype(jnp.bfloat16)
    layer_out = (
        resid1 + jnp.dot(gelu_low, w_down, preferred_element_type=jnp.float32) + small_weight[5]
    ).astype(jnp.bfloat16)
    grad_out = out_grad.reshape(rows_total, width)
    grad_down = jnp.einsum("rf,rd->fd", gelu_low, grad_out, preferred_element_type=jnp.float32)
    bias_down = jnp.sum(grad_out, axis=0, dtype=jnp.float32)
    grad_gelu = jnp.einsum("rd,fd->rf", grad_out, w_down, preferred_element_type=jnp.float32)
    grad_pre = gelu_pull(grad_gelu)[0].astype(jnp.bfloat16)
    grad_up = jnp.einsum("rd,rf->df", act2, grad_pre, preferred_element_type=jnp.float32)
    bias_up = jnp.sum(grad_pre, axis=0, dtype=jnp.float32)
    grad_act2 = jnp.einsum("rf,df->rd", grad_pre, w_up, preferred_element_type=jnp.float32)
    back_resid, gain2_grad, shift2_grad = norm2_pull(grad_act2)
    grad_resid1 = grad_out.astype(jnp.float32) + back_resid
    grad_branch = grad_resid1.astype(jnp.bfloat16)
    grad_wout = jnp.einsum("rd,re->de", mixed_flat, grad_branch, preferred_element_type=jnp.float32)
    grad_mixed = jnp.einsum(
        "re,de->rd", grad_branch, w_out, preferred_element_type=jnp.float32
    ).astype(jnp.bfloat16)
    grad_query, key_terms, value_terms = lax.map(
        attend_backward,
        (
            query_tables,
            keys_all,
            values_all,
            grad_mixed.reshape(local_tables, 2 * quarter_rows, width),
            log_totals,
        ),
    )
    key_sums, value_sums = (
        lax.psum_scatter(
            key_terms.astype(jnp.bfloat16), "feat", scatter_dimension=1, tiled=True
        ).astype(jnp.float32),
        lax.psum_scatter(
            value_terms.astype(jnp.bfloat16), "feat", scatter_dimension=1, tiled=True
        ).astype(jnp.float32),
    )
    grad_keys = key_sums.astype(jnp.bfloat16)
    grad_values = value_sums.astype(jnp.bfloat16)
    grad_query = grad_query.reshape(rows_total, width)
    grad_wq = jnp.einsum("rd,re->de", act1, grad_query, preferred_element_type=jnp.float32)
    grad_wk = jnp.einsum("tjd,tje->de", support, grad_keys, preferred_element_type=jnp.float32)
    grad_wv = jnp.einsum("tjd,tje->de", support, grad_values, preferred_element_type=jnp.float32)
    grad_act1 = jnp.einsum(
        "re,de->rd", grad_query, w_query, preferred_element_type=jnp.float32
    ).reshape(local_tables, 2, quarter_rows, width)
    support_back = jnp.einsum(
        "tje,de->tjd", grad_keys, w_key, preferred_element_type=jnp.float32
    ) + jnp.einsum("tje,de->tjd", grad_values, w_value, preferred_element_type=jnp.float32)
    grad_act1 = grad_act1.at[:, 0].add(support_back)
    back_hidden, gain1_grad, shift1_grad = norm1_pull(grad_act1.reshape(rows_total, width))
    grad_hidden = grad_resid1 + back_hidden
    bias_embed = jnp.sum(grad_hidden, axis=0)
    grad_embed = grad_hidden.astype(jnp.bfloat16).reshape(row_shape)
    whole_terms = jnp.einsum(
        "tshf,tshd->fd", rows_features, grad_embed, preferred_element_type=jnp.float32
    )
    emb_terms = lax.psum_scatter(
        whole_terms.astype(jnp.bfloat16), "feat", scatter_dimension=0, tiled=True
    ).astype(jnp.float32)
    row_inputs = jnp.einsum(
        "tshd,fd->tshf", grad_embed, emb_whole, preferred_element_type=jnp.float32
    ).astype(jnp.bfloat16)
    returned = lax.all_to_all(row_inputs, "feat", split_axis=3, concat_axis=2, tiled=True)
    grad_inputs = returned * mask_local[:, None, None, :].astype(jnp.bfloat16)
    grad_stack = jnp.concatenate(
        [
            jnp.stack([grad_wq, grad_wk, grad_wv, grad_wout]),
            grad_up.reshape(width, 4, width).transpose(1, 0, 2),
            grad_down.reshape(4, width, width),
        ],
        axis=0,
    )
    small_terms = jnp.concatenate(
        [
            jnp.stack([bias_embed, gain1_grad, shift1_grad, gain2_grad, shift2_grad, bias_down]),
            bias_up.reshape(4, width),
        ],
        axis=0,
    )
    layer_sum, small_grad = lax.psum((grad_stack, small_terms), ("feat", "rows"))
    embed_sum = lax.psum(emb_terms, "rows")
    unit_grads = layer_sum.reshape(unit_count, block_rows, width)
    slot_grads = jnp.einsum("ci,ixy->cxy", selector, unit_grads, precision=HIGH)
    first_slots, second_slots, weight_new = adamw(
        weight_slots, slot_grads, moment1_slots, moment2_slots, RATE_MATRIX
    )
    small_first, small_second, small_new = adamw(
        small_weight, small_grad, small_moment1, small_moment2, RATE_SMALL
    )
    occupied = jnp.sum(selector, axis=1)[:, None, None]
    weight_new = weight_new * occupied
    emb_first, emb_second, emb_new = adamw(
        emb_weight, embed_sum, emb_moment1, emb_moment2, RATE_EMBED
    )
    return (
        layer_out.reshape(row_shape),
        grad_inputs,
        slot_grads * occupied,
        first_slots * occupied,
        second_slots * occupied,
        weight_new,
        weight_new.astype(jnp.bfloat16),
        embed_sum,
        emb_first,
        emb_second,
        emb_new,
        emb_new.astype(jnp.bfloat16),
        small_grad,
        small_first,
        small_second,
        small_new,
    )


def solution(mesh):
    in_specs = (
        P("rows", None, None, "feat"),
        P(None, "feat"),
        P("rows"),
        P(),
        P("rows", None, "feat", None),
        P("rows", None, None),
        P("rows", None, None),
        P("rows", None, None),
        P("feat", None),
        P("feat", None),
        P("feat", None),
        P(),
        P(),
        P(),
    )
    out_specs = (
        P("rows", None, "feat", None),
        P("rows", None, None, "feat"),
        P("rows", None, None),
        P("rows", None, None),
        P("rows", None, None),
        P("rows", None, None),
        P("rows", None, None),
        P("feat", None),
        P("feat", None),
        P("feat", None),
        P("feat", None),
        P("feat", None),
        P(),
        P(),
        P(),
        P(),
    )
    return jax.shard_map(body, mesh=mesh, in_specs=in_specs, out_specs=out_specs, check_vma=False)
```

profile of v0, /device:TPU:0, one launch (start us, length us, event | category | flops | bytes accessed | tf_op | source)
XLA Modules:
  0.0 651.3 jit_solution(3282295130036290743)
XLA Ops:
  16.0 4.2 all-to-all-start
  21.0 6.1 all-gather
  36.9 101.4 %all-gather.5.cloned.1.call-done = bf16[32,256,512]{2,1,0:T(8,128)(2,1)} async-done(((bf16[4,256,512]{2,1,0:T(8,128)(2,1)}), bf16[32,256,512]{2,1,0:T(8,128)(2,1)}) %all-gather.5.cloned.1.call-update) | async-done | bytes 8388624 | tf_op jit(solution)/shard_map/all_gather | solution.py:132
  138.4 9.6 %fusion.48 = bf16[24,256,512]{2,0,1:T(8,128)(2,1)S(1)} fusion(bf16[32,256,512]{2,1,0:T(8,128)(2,1)} %all-gather.5.cloned.1.call-done, s32[24]{0:T(128)S(1)} %multiply_add_fusion.5), kind=kOutput, calls=%fused_computation.87 | convolution fusion | flops 204473088 | bytes 14680160 | tf_op jit(solution)/shard_map/ic,cxy->ixy/dot_general | solution.py:136
  159.8 4.3 fusion.101
  166.1 4.2 copy.322
  173.3 3.8 copy.323
  181.0 3.9 copy.318
  185.0 15.9 %all-gather.7.cloned.1.call-done = bf16[2,1024,512]{2,1,0:T(8,128)(2,1)} async-done(((bf16[2,256,512]{2,1,0:T(8,128)(2,1)}), bf16[2,1024,512]{2,1,0:T(8,128)(2,1)}) %all-gather.7.cloned.1.call-update) | async-done | bytes 2097168 | tf_op jit(solution)/shard_map/all_gather | solution.py:172
  200.9 3.9 copy.316
  205.8 19.4 %while.27 = (s32[]{:T(128)}, bf16[2,512,512]{2,1,0:T(8,128)(2,1)}, f32[2,4,512]{2,1,0:T(4,128)S(1)}, bf16[2,1024,512]{1,2,0:T(8,128)(2,1)}, bf16[2,512,512]{1,2,...) while((s32[]{:T(128)}, bf16[2,512,512]{2,1,0:T(8,128)(2,1)}, f32[2,4,512]{2,1,0:T(4,128)S(1)}, ...), condition=%wide.region_6.7_spmd, body=%wide.region_3.6_spmd.sunk | while | flops 1092876288 | bytes 35717220 | solution.py:175
  227.9 20.7 %fusion.12 = (f32[1024,2048]{1,0:T(8,128)S(1)}, f32[1024,2048]{1,0:T(8,128)S(1)}) fusion(f32[2048]{0:T(1024)S(1)} %bitcast.389, bf16[512,2048]{0,1:T(8,128)(2,1)} %bitcast.378, f32[1024,512]{1,0:T(8,128)S(1)} %get-tuple-element.388, f32[512]{0:T(512)S(1)} %bitcast.402, f32[512]{0:T(512)S(1)} %bitcast.398, f32[1024]{0:T(1024)S(1)} %fusion.78, ...), kind=kOutput, calls=%fused_computation.33 | convolution fusion | flops 2282225664 | bytes 20992000 | tf_op jit(solution)/shard_map/dot_general | solution.py:180
  248.6 5.8 convert_reduce_fusion
  254.4 6.5 multiply_reduce_fusion.2
  266.2 36.3 %while.28 = (s32[]{:T(128)}, bf16[2,512,512]{2,1,0:T(8,128)(2,1)}, bf16[2,1024,512]{1,2,0:T(8,128)(2,1)}, bf16[2,1024,512]{1,2,0:T(8,128)(2,1)}, bf16[2,1024,512...) while((s32[]{:T(128)}, bf16[2,512,512]{2,1,0:T(8,128)(2,1)}, ...), condition=%wide.region_13.14_spmd, body=%wide.region_11.13_spmd.sunk | while | flops 2711091200 | bytes 84467848 | solution.py:203
  292.7 2.9 multiply_reduce_fusion.11
  303.2 20.8 %fusion.15 = bf16[2048,1024]{0,1:T(8,128)(2,1)} fusion(f32[1024,2048]{1,0:T(8,128)} %copy-done.4, f32[2048]{0:T(1024)S(1)} %bitcast.391), kind=kLoop, calls=%fused_computation.36 | loop fusion | flops 138412032 | bytes 12591104 | tf_op jit(solution)/shard_map/convert_element_type | solution.py:184
  324.0 6.8 %copy.365 = bf16[2048,1024]{1,0:T(8,128)(2,1)} copy(bf16[2048,1024]{0,1:T(8,128)(2,1)} %fusion.15) | data formatting | bytes 8388608 | tf_op jit(solution)/shard_map/rf,rd->fd/dot_general | solution.py:189
  330.8 3.0 fusion.60
  333.8 6.8 %fusion.92 = f32[512,2048]{1,0:T(8,128)} fusion(bf16[1024,2048]{1,0:T(8,128)(2,1)} %copy-done.9, f32[1024,512]{1,0:T(8,128)S(1)} %copy-done.3, f32[512]{0:T(512)S(1)} %bitcast.403, f32[512]{0:T(512)S(1)} %bitcast.401, f32[1024]{0:T(1024)S(1)} %fusion.78, f32[1024]{0:T(1024)S(1)} %broadcast_multiply_fusion.4), kind=kOutput, calls=%fused_computation.192 | convolution fusion | flops 2150105088 | bytes 10498048 | tf_op jit(solution)/shard_map/rd,rf->df/dot_general | solution.py:193
  343.1 25.1 %reduce-scatter.7.cloned.1.call-done = bf16[2,256,512]{1,2,0:T(8,128)(2,1)} async-done(((bf16[2,1024,512]{1,2,0:T(8,128)(2,1)}), bf16[2,256,512]{1,2,0:T(8,128)(2,1)}) %reduce-scatter.7.cloned.1.call-update) | async-done | bytes 524304 | tf_op jit(solution)/shard_map/reduce_scatter | solution.py:217
  371.0 3.6 fusion.57
  377.2 4.4 convolution_dynamic-update-slice_fusion
  381.6 16.6 %copy.341 = f32[24,256,512]{2,0,1:T(8,128)} copy(f32[24,256,512]{2,1,0:T(8,128)} %bitcast.357) | data formatting | bytes 25165824 | tf_op jit(solution)/shard_map/reshape | solution.py:266
  402.6 10.8 %add_convert_fusion = bf16[1024,512]{1,0:T(8,128)(2,1)} fusion(f32[1024,512]{1,0:T(8,128)S(1)} %copy-done.3, bf16[2048,512]{1,0:T(8,128)(2,1)} %bitcast.361, f32[1024,2048]{1,0:T(8,128)} %copy-done.13, f32[1024,2048]{1,0:T(8,128)} %copy-done.4, f32[2048]{0:T(1024)S(1)} %bitcast.392, f32[512]{0:T(512)S(1)} %bitcast.414), kind=kOutput, calls=%fused_computation.110 | convolution fusion | flops 2157445120 | bytes 22030336 | tf_op jit(solution)/shard_map/dot_general | solution.py:186
  419.3 3.4 all-to-all-start.1
  423.0 9.1 %fusion = bf16[32,512]{1,0:T(8,128)(2,1)S(1)} fusion(bf16[100,512]{1,0:T(8,128)(2,1)S(1)} %fusion.65), kind=kCustom, calls=%all-reduce-scatter | all-reduce-scatter fusion | flops 65537 | bytes 135680
  433.7 42.6 %psum.23 = f32[10,512]{1,0:T(8,128)S(1)} all-reduce(f32[10,512]{1,0:T(8,128)S(1)} %concatenate.9), channel_id=1, replica_groups=mesh['feat'=4,'rows'=8] {'feat','rows'}, use_global_device_ids=true, to_apply=%region_29.30 | all-reduce | flops 5120 | bytes 40960 | tf_op jit(solution)/shard_map/psum | solution.py:264
  477.2 37.7 %psum.22 = f32[25,512]{1,0:T(8,128)S(1)} all-reduce(f32[25,512]{1,0:T(8,128)S(1)} %dynamic-slice_convert_fusion), channel_id=1, replica_groups=mesh['feat'=4,'rows'=8] {'rows'}, use_global_device_ids=true, to_apply=%region_21.22 | all-reduce | flops 12800 | bytes 102400 | tf_op jit(solution)/shard_map/psum | solution.py:265
  516.9 113.6 %all-reduce.4.cloned.1.call-done = f32[24,256,512]{2,0,1:T(8,128)} async-done(((f32[24,256,512]{2,0,1:T(8,128)}), f32[24,256,512]{2,0,1:T(8,128)}) %all-reduce.4.cloned.1.call-update) | async-done | bytes 12582928 | tf_op jit(solution)/shard_map/psum | solution.py:264
  630.5 7.4 %fusion.80 = f32[4,256,512]{2,0,1:T(4,128)S(1)} fusion(f32[24,256,512]{2,0,1:T(8,128)} %all-reduce.4.cloned.1.call-done, s32[24]{0:T(128)S(1)} %copy-done.62, pred[24]{0:T(512)(128)(4,1)S(1)} %broadcast_compare_fusion), kind=kOutput, calls=%fused_computation.179 | convolution fusion | flops 150995136 | bytes 14680184 | tf_op jit(solution)/shard_map/ci,ixy->cxy/dot_general | solution.py:267
  637.9 6.3 fusion.99
  (269 shorter events, 123.8 us)
Async XLA Ops:
  7.2 131.2 %all-gather.5.cloned.1.call-start = ((), (), s32[]{:S(2)}) async-start(), calls=%async_computation.4 | async-start | bytes 9437184 | tf_op jit(solution)/shard_map/all_gather | solution.py:132
  16.0 14.3 %all-to-all-start = ((bf16[4,2,12800]{2,1,0:T(2,128)(2,1)}), bf16[4,2,12800]{2,1,0:T(2,128)(2,1)S(1)}, u32[]{:S(2)}, u32[]{:S(2)}) async-start(bf16[4,2,12800]{2,1,0:T(2,128)(2,1)} %reshape.451), calls=%async_computation | async-start | bytes 409600 | tf_op jit(solution)/shard_map/all_to_all | solution.py:150
  20.2 160.9 %all-gather.9.cloned.1.call-start = ((), (), s32[]{:S(2)}) async-start(), calls=%async_computation.6 | async-start | bytes 2621440 | tf_op jit(solution)/shard_map/all_gather | solution.py:171
  29.6 118.4 %copy-start.42 = (f32[1,512]{1,0:T(1,128)}, f32[1,512]{1,0:T(1,128)S(1)}, u32[]{:S(2)}) copy-start(f32[1,512]{1,0:T(1,128)S(1)} %get-tuple-element.377) | copy-start | bytes 6148
  29.6 198.2 %copy-start.52 = (f32[1,512]{1,0:T(1,128)}, f32[1,512]{1,0:T(1,128)S(1)}, u32[]{:S(2)}) copy-start(f32[1,512]{1,0:T(1,128)S(1)} %get-tuple-element.374) | copy-start | bytes 6148
  34.8 190.4 %copy-start = (f32[2,2,256,512]{3,2,1,0:T(8,128)}, f32[2,2,256,512]{3,2,1,0:T(8,128)S(1)}, u32[]{:S(2)}) copy-start(f32[2,2,256,512]{3,2,1,0:T(8,128)S(1)} %get-tuple-element.386) | copy-start | bytes 6291460
  36.9 140.2 %copy-start.17 = (bf16[2,2,256,512]{3,2,1,0:T(8,128)(2,1)}, bf16[2,2,256,512]{3,2,1,0:T(8,128)(2,1)S(1)}, u32[]{:S(2)}) copy-start(bf16[2,2,256,512]{3,2,1,0:T(8,128)(2,1)S(1)} %add_convert_fusion.2) | copy-start | bytes 3145732
  155.2 45.7 %all-gather.7.cloned.1.call-start = ((), (), s32[]{:S(2)}) async-start(), calls=%async_computation.5 | async-start | bytes 2621440 | tf_op jit(solution)/shard_map/all_gather | solution.py:172
  158.4 182.2 %reduce-scatter.5.cloned.1.call-start = ((), (), s32[]{:S(2)}) async-start(), calls=%async_computation.7 | async-start | bytes 2621440 | tf_op jit(solution)/shard_map/reduce_scatter | solution.py:214
  227.4 33.5 %copy-start.2 = (f32[1024,512]{1,0:T(8,128)}, f32[1024,512]{1,0:T(8,128)S(1)}, u32[]{:S(2)}) copy-start(f32[1024,512]{1,0:T(8,128)S(1)} %get-tuple-element.388) | copy-start | bytes 6291460
  227.9 20.7 %copy-start.10 = (bf16[2,2,256,512]{3,2,1,0:T(8,128)(2,1)S(1)}, bf16[2,2,256,512]{3,2,1,0:T(8,128)(2,1)}, u32[]{:S(2)}) copy-start(bf16[2,2,256,512]{3,2,1,0:T(8,128)(2,1)} %param.24) | copy-start | bytes 3145732
  227.9 20.7 %copy-start.14 = (bf16[8,256,512]{2,1,0:T(8,128)(2,1)S(1)}, bf16[8,256,512]{2,1,0:T(8,128)(2,1)}, u32[]{:S(2)}) copy-start(bf16[8,256,512]{2,1,0:T(8,128)(2,1)} %copy.323) | copy-start | bytes 6291460
  302.6 65.6 %reduce-scatter.7.cloned.1.call-start = ((), (), s32[]{:S(2)}) async-start(), calls=%async_computation.8 | async-start | bytes 2621440 | tf_op jit(solution)/shard_map/reduce_scatter | solution.py:217
  303.1 27.6 %copy-start.15 = (bf16[2,512,512]{2,1,0:T(8,128)(2,1)S(1)}, bf16[2,512,512]{2,1,0:T(8,128)(2,1)}, u32[]{:S(2)}) copy-start(bf16[2,512,512]{2,1,0:T(8,128)(2,1)} %get-tuple-element.112) | copy-start | bytes 3145732
  303.2 327.3 %all-reduce.4.cloned.1.call-start = ((), (), s32[]{:S(2)}) async-start(), calls=%async_computation.9 | async-start | bytes 25165824 | tf_op jit(solution)/shard_map/psum | solution.py:264
  343.1 34.1 %copy-start.11 = (bf16[2,2,256,512]{3,2,1,0:T(8,128)(2,1)S(1)}, bf16[2,2,256,512]{3,2,1,0:T(8,128)(2,1)}, u32[]{:S(2)}) copy-start(bf16[2,2,256,512]{3,2,1,0:T(8,128)(2,1)} %param.24) | copy-start | bytes 3145732
  402.6 11.9 %copy-start.1 = (f32[2,2,256,512]{3,2,1,0:T(8,128)S(1)}, f32[2,2,256,512]{3,2,1,0:T(8,128)}, u32[]{:S(2)}) copy-start(f32[2,2,256,512]{3,2,1,0:T(8,128)} %copy-done) | copy-start | bytes 6291460
  402.6 11.9 %copy-start.38 = (f32[2,2,256]{2,1,0:T(2,128)S(1)}, f32[2,2,256]{2,1,0:T(2,128)}, u32[]{:S(2)}) copy-start(f32[2,2,256]{2,1,0:T(2,128)} %copy-done.37) | copy-start | bytes 12292
  415.1 18.4 %copy-start.59 = (f32[512]{0:T(512)S(1)}, f32[512]{0:T(512)}, u32[]{:S(2)}) copy-start(f32[512]{0:T(512)} %get-tuple-element.309) | copy-start | bytes 6148
  415.1 18.4 %copy-start.60 = (f32[512]{0:T(512)S(1)}, f32[512]{0:T(512)}, u32[]{:S(2)}) copy-start(f32[512]{0:T(512)} %get-tuple-element.311) | copy-start | bytes 6148
  415.2 61.1 %copy-start.39 = (f32[10,512]{1,0:T(8,128)S(1)}, f32[10,512]{1,0:T(8,128)}, u32[]{:S(2)}) copy-start(f32[10,512]{1,0:T(8,128)} %param.31) | copy-start | bytes 61444
  415.2 61.1 %copy-start.50 = (f32[10,512]{1,0:T(8,128)S(1)}, f32[10,512]{1,0:T(8,128)}, u32[]{:S(2)}) copy-start(f32[10,512]{1,0:T(8,128)} %param.33) | copy-start | bytes 61444
  415.2 61.1 %copy-start.51 = (f32[10,512]{1,0:T(8,128)S(1)}, f32[10,512]{1,0:T(8,128)}, u32[]{:S(2)}) copy-start(f32[10,512]{1,0:T(8,128)} %param.32) | copy-start | bytes 61444
  415.2 99.7 %copy-start.34 = (f32[25,512]{1,0:T(8,128)S(1)}, f32[25,512]{1,0:T(8,128)}, u32[]{:S(2)}) copy-start(f32[25,512]{1,0:T(8,128)} %param.28) | copy-start | bytes 153604
  415.2 99.7 %copy-start.40 = (f32[25,512]{1,0:T(8,128)S(1)}, f32[25,512]{1,0:T(8,128)}, u32[]{:S(2)}) copy-start(f32[25,512]{1,0:T(8,128)} %param.30) | copy-start | bytes 153604
  415.3 99.7 %copy-start.41 = (f32[25,512]{1,0:T(8,128)S(1)}, f32[25,512]{1,0:T(8,128)}, u32[]{:S(2)}) copy-start(f32[25,512]{1,0:T(8,128)} %param.29) | copy-start | bytes 153604
  415.3 100.6 %copy-start.58 = (bf16[2,25]{1,0:T(2,128)(2,1)S(1)}, bf16[2,25]{1,0:T(2,128)(2,1)}, u32[]{:S(2)}) copy-start(bf16[2,25]{1,0:T(2,128)(2,1)} %copy-done.57) | copy-start | bytes 304
  419.3 96.4 %all-to-all-start.1 = ((bf16[2,2,256,100]{2,1,0,3:T(2,128)(2,1)}), bf16[2,2,256,100]{2,1,0,3:T(2,128)(2,1)S(1)}, u32[]{:S(2)}, u32[]{:S(2)}) async-start(bf16[2,2,256,100]{2,1,0,3:T(2,128)(2,1)} %copy.331), calls=%async_computation.3 | async-start | bytes 409600 | tf_op jit(solution)/shard_map/all_to_all | solution.py:247
  432.2 44.8 %collective-permute-start = (bf16[21,512]{1,0:T(8,128)(2,1)S(1)}, bf16[21,512]{1,0:T(8,128)(2,1)S(1)}, u32[]{:S(2)}, u32[]{:S(2)}) collective-permute-start(bf16[21,512]{1,0:T(8,128)(2,1)S(1)} %slice.101), channel_id=1, source_target_pairs={{0,8},{8,16},{16,24},{1,9},{9,17},{17,25},{2,10},{10,18},{18,26},{... | collective-permute-start | bytes 64520
  476.3 161.5 %copy-start.36 = (f32[10,512]{1,0:T(8,128)}, f32[10,512]{1,0:T(8,128)S(1)}, u32[]{:S(2)}) copy-start(f32[10,512]{1,0:T(8,128)S(1)} %psum.23) | copy-start | bytes 61444
  477.0 160.9 %copy-start.12 = (f32[4,256,512]{2,1,0:T(8,128)S(1)}, f32[4,256,512]{2,1,0:T(8,128)}, u32[]{:S(2)}) copy-start(f32[4,256,512]{2,1,0:T(8,128)} %param.25) | copy-start | bytes 6291460
  515.0 129.2 %copy-start.35 = (f32[25,512]{1,0:T(8,128)}, f32[25,512]{1,0:T(8,128)S(1)}, u32[]{:S(2)}) copy-start(f32[25,512]{1,0:T(8,128)S(1)} %psum.22) | copy-start | bytes 153604
  (42 other events, 203.7 us)
Sparse Core Ops, SparseCore 0:
  10.7 127.6 all-gather.4
  155.3 20.7 all-gather.8
  178.3 22.5 all-gather.6
  302.7 31.4 reduce-scatter.4
  336.7 31.4 reduce-scatter.6
  398.3 232.0 all-reduce.3
where the time goes:
time: 656 us; the launch traced here: 651 us
  waiting for transfers between devices  257 us (39%)
  matrix products  122 us (19%)
  local copies, waits for them, and re-layouts  101 us (15%)
  blocking collectives  95.6 us (15%)
  other arithmetic  50.2 us (8%)
  between operations  16.1 us (2%)
  starting transfers between devices  9.63 us (1%)
    psum x1, waiting for transfers between devices, body(): lax.psum((grad_stack, small_terms), ('feat', 'rows'))  114 us
    all_gather x1, waiting for transfers between devices, body(): lax.all_gather(weight_slots.astype(jnp.bfloat16), 'rows', axis=0, tiled=T...  101 us
    psum x1, blocking collectives, body(): lax.psum((grad_stack, small_terms), ('feat', 'rows'))  42.6 us
    psum x1, blocking collectives, body(): embed_sum = lax.psum(emb_terms, 'rows')  37.7 us
    reduce_scatter x1, waiting for transfers between devices, body(): lax.psum_scatter(value_terms.astype(jnp.bfloat16), 'feat', scatter_dimens...  25.1 us
    convert_element_type x1, other arithmetic, body(): gelu_low = gelu_out.astype(jnp.bfloat16)  20.8 us
    dot_general x1, matrix products, body(): jnp.dot(act2, w_up, preferred_element_type=jnp.float32)  20.7 us
    unnamed x143, local copies, waits for them, and re-layouts  16.7 us
  transfers between devices with their start and end apart: 9, of which 4 were waited for; matrix products, arithmetic and copies ran while one was open for 18% of the time, Pallas kernels for 0%

commit v1 on v0

--- a/solution.py
+++ b/solution.py
@@ -1,7 +1,106 @@
+import functools
 import jax
 import jax.numpy as jnp
 from jax import lax
 from jax.sharding import PartitionSpec as P
+from jax.experimental import pallas as pl
+from jax.experimental.pallas import tpu as pltpu
+
+MESH = pl.DeviceIdType.MESH
+
+def gather_kernel(R, slots_ref, G_ref, own, lsem, hs, hr, xs, xr, cs, cr, c2s, c2r):
+    f = lax.axis_index("feat")
+    r = lax.axis_index("rows")
+    x = f // 2
+    c = f % 2
+    n = R.bit_length() - 1
+    S, BR, W = own.shape
+    BH, CH = BR // 2, W // 2
+    core_id = (f ^ 1, r)
+    x_id = (f ^ 2, r)
+    row_id = [(f, r ^ (1 << (n - 1 - j))) for j in range(n)]
+    bar = pltpu.get_barrier_semaphore()
+    peers = [core_id, x_id] + row_id
+    for d in peers:
+        pl.semaphore_signal(bar, inc=1, device_id=d, device_id_type=MESH)
+    own[...] = slots_ref[...].astype(jnp.bfloat16)
+    pl.semaphore_wait(bar, len(peers))
+    local = pltpu.make_async_copy(own, G_ref.at[0], lsem)
+    local.start()
+    subs = [(j, g) for j in range(n) for g in range(-1, j)]
+    index = {jg: i for i, jg in enumerate(subs)}
+
+    def span(g):
+        return (0, 1) if g < 0 else (1 << g, 1 << g)
+
+    def region(s, half_row, half_col):
+        rows = pl.ds(pl.multiple_of(half_row * BH, BH), BH)
+        cols = pl.ds(0, W) if s == 0 else pl.ds(pl.multiple_of(half_col * CH, CH), CH)
+        return rows, cols
+
+    def hyper(s, j, g):
+        rows, cols = region(s, c, x)
+        start, size = span(g)
+        src = own.at[pl.ds(s, 1), rows, cols] if g < 0 else G_ref.at[pl.ds(start, size), s, rows, cols]
+        k = index[(j, g)]
+        return pltpu.make_async_remote_copy(
+            src_ref=src,
+            dst_ref=G_ref.at[pl.ds((1 << j) + start, size), s, rows, cols],
+            send_sem=hs.at[s, k], recv_sem=hr.at[s, k], device_id=row_id[j], device_id_type=MESH)
+
+    def forward(s, j, g, half_col, sems, semr, dev):
+        rows, cols = region(s, c, half_col)
+        start, size = span(g)
+        k = index[(j, g)]
+        ref = G_ref.at[pl.ds((1 << j) + start, size), s, rows, cols]
+        return pltpu.make_async_remote_copy(src_ref=ref, dst_ref=ref, send_sem=sems.at[s, k], recv_sem=semr.at[s, k], device_id=dev, device_id_type=MESH)
+
+    order = [1, 2, 3, 0]
+    for s in order:
+        for j in range(n):
+            hyper(s, j, -1).start()
+    def x_arrive(j):
+        for s in order:
+            if s == 0:
+                continue
+            for g in range(-1, j):
+                forward(s, j, g, x, xs, xr, x_id).wait_recv()
+                forward(s, j, g, 1 - x, c2s, c2r, core_id).start()
+    for j in range(n):
+        for s in order:
+            for g in range(-1, j):
+                hyper(s, j, g).wait_recv()
+                if s > 0:
+                    forward(s, j, g, x, xs, xr, x_id).start()
+                forward(s, j, g, x, cs, cr, core_id).start()
+            for j2 in range(j + 1, n):
+                hyper(s, j2, j).start()
+        if j > 0:
+            x_arrive(j - 1)
+    x_arrive(n - 1)
+    local.wait()
+    for s in order:
+        for (j, g) in subs:
+            hyper(s, j, g).wait_send()
+            forward(s, j, g, x, cs, cr, core_id).wait()
+            if s > 0:
+                forward(s, j, g, x, xs, xr, x_id).wait_send()
+                forward(s, j, g, 1 - x, c2s, c2r, core_id).wait()
+
+def gather_weights(R, slots):
+    S, BR, W = slots.shape
+    n = R.bit_length() - 1
+    M = n * (n + 1) // 2
+    sem = pltpu.SemaphoreType.DMA((S, M))
+    return pl.pallas_call(
+        functools.partial(gather_kernel, R),
+        out_shape=jax.ShapeDtypeStruct((R, S, BR, W), jnp.bfloat16),
+        in_specs=[pl.BlockSpec(memory_space=pltpu.VMEM)],
+        out_specs=pl.BlockSpec(memory_space=pl.ANY),
+        scratch_shapes=[pltpu.VMEM((S, BR, W), jnp.bfloat16), pltpu.SemaphoreType.DMA] + [sem] * 8,
+        compiler_params=pltpu.CompilerParams(collective_id=0, has_side_effects=True, vmem_limit_bytes=56 * 2**20),
+        name="gather_weights",
+    )(slots)
 
 HEADS = 4
 HEAD_DIM = 128
@@ -128,13 +227,16 @@
     selector = ((owners[None, :] == my_row) & (owner_rank[None, :] == slot_iota)).astype(
         jnp.float32
     )
-    slot_ids = owners * capacity + owner_rank
-    piece = lax.all_gather(weight_slots.astype(jnp.bfloat16), "rows", axis=0, tiled=True)
-    count = piece.shape[0]
-    piece_iota = lax.broadcasted_iota(jnp.int32, (unit_count, count), 1)
-    picks = (slot_ids[:, None] == piece_iota).astype(jnp.bfloat16)
-    gathered = jnp.einsum("ic,cxy->ixy", picks, piece, preferred_element_type=jnp.float32)
-    matrices = gathered.reshape(-1, width, width).astype(jnp.bfloat16)
+    row_count = lax.axis_size("rows")
+    piece = gather_weights(row_count, weight_slots)
+    distance = owners ^ my_row
+    place = jnp.zeros_like(distance)
+    bits = row_count.bit_length() - 1
+    for bit in range(bits):
+        place = place | (((distance >> bit) & 1) << (bits - 1 - bit))
+    flat_ids = place * capacity + owner_rank
+    pieces = piece.reshape(row_count * capacity, block_rows, width)
+    matrices = jnp.take(pieces, flat_ids, axis=0).reshape(-1, width, width)
     w_query = matrices[0]
     w_key = matrices[1]
     w_value = matrices[2]

time: 656 us -> 609 us (0.928)
  waiting for transfers between devices: 257 us -> 165 us
  Pallas kernels: 0 us -> 52.8 us
    all_gather x1 -> x0, waiting for transfers between devices: 101 us -> none  [body(): lax.all_gather(weight_slots.astype(jnp.bfloat16), 'rows', axis=0, tiled=T...]
    pallas_call x0 -> x1, Pallas kernels: none -> 52.8 us  [gather_weights(): pl.pallas_call(functools.partial(gather_kernel, R), out_shape=jax.ShapeDt...]
    dot_general x1 -> x0, matrix products: 9.62 us -> none  [body(): jnp.einsum('ic,cxy->ixy', picks, piece, preferred_element_type=jnp.float32)]
    gather x0 -> x1, local copies, waits for them, and re-layouts: none -> 7.87 us  [body(): matrices = jnp.take(pieces, flat_ids, axis=0).reshape(-1, width, width)]
    unnamed x143 -> x139, local copies, waits for them, and re-layouts: 16.7 us -> 13.9 us
  transfers between devices with their start and end apart: 9 -> 8, of which waited for: 4 -> 4; matrix products, arithmetic and copies ran while one was open for 18% -> 18% of each run, Pallas kernels for 0% -> 9%
where the time goes in v1:
time: 609 us; the launch traced here: 600 us
  waiting for transfers between devices  165 us (27%)
  matrix products  116 us (19%)
  blocking collectives  94.9 us (16%)
  local copies, waits for them, and re-layouts  94.5 us (16%)
  Pallas kernels  52.8 us (9%)
  other arithmetic  51.5 us (8%)
  between operations  15.7 us (3%)
  starting transfers between devices  9.53 us (2%)
    psum x1, waiting for transfers between devices, body(): lax.psum((grad_stack, small_terms), ('feat', 'rows'))  114 us
    pallas_call x1, Pallas kernels, gather_weights(): pl.pallas_call(functools.partial(gather_kernel, R), out_shape=jax.ShapeDt...  52.8 us
    psum x1, blocking collectives, body(): lax.psum((grad_stack, small_terms), ('feat', 'rows'))  42.8 us
    psum x1, blocking collectives, body(): embed_sum = lax.psum(emb_terms, 'rows')  37.4 us
    reduce_scatter x1, waiting for transfers between devices, body(): lax.psum_scatter(value_terms.astype(jnp.bfloat16), 'feat', scatter_dimens...  24.8 us
    all_gather x1, waiting for transfers between devices, body(): lax.all_gather(values_local, 'feat', axis=1, tiled=True)  20.8 us
    convert_element_type x1, other arithmetic, body(): gelu_low = gelu_out.astype(jnp.bfloat16)  20.8 us
    dot_general x1, matrix products, body(): jnp.dot(act2, w_up, preferred_element_type=jnp.float32)  20.6 us
  transfers between devices with their start and end apart: 8, of which 4 were waited for; matrix products, arithmetic and copies ran while one was open for 18% of the time, Pallas kernels for 9%

profile of v1, /device:TPU:0, one launch (start us, length us, event | category | flops | bytes accessed | tf_op | source)
XLA Modules:
  0.0 600.3 jit_solution(7327129926518412998)
XLA Ops:
  13.2 4.2 all-to-all-start
  20.4 5.7 all-gather
  26.1 52.8 %gather_weights.1 = bf16[8,4,256,512]{3,2,1,0:T(8,128)(2,1)} custom-call(f32[4,256,512]{2,1,0:T(8,128)} %slots_ref.1), custom_call_target="tpu_custom_call" | custom-call | tf_op jit(solution)/shard_map/gather_weights/pallas_call | solution.py:95
  78.9 7.9 %gather_fusion = bf16[24,256,512]{2,1,0:T(8,128)(2,1)} fusion(bf16[32,256,512]{2,1,0:T(8,128)(2,1)} %bitcast.353, s32[1024]{0:T(1024)S(1)} %pad_clamp_fusion), kind=kCustom, calls=%fused_computation | custom fusion | bytes 12583008 | tf_op jit(solution)/shard_map/jit(_take)/gather | solution.py:239
  86.8 3.5 broadcast_select_fusion
  106.8 4.6 fusion.93
  111.4 4.2 copy.279
  120.6 5.0 all-gather.6.cloned.1.call-done
  125.6 3.9 copy.277
  129.5 20.8 %all-gather.4.cloned.1.call-done = bf16[2,1024,512]{2,1,0:T(8,128)(2,1)} async-done(((bf16[2,256,512]{2,1,0:T(8,128)(2,1)}), bf16[2,1024,512]{2,1,0:T(8,128)(2,1)}) %all-gather.4.cloned.1.call-update) | async-done | bytes 2097168 | tf_op jit(solution)/shard_map/all_gather | solution.py:274
  150.4 3.9 copy.275
  155.3 19.3 %while.27 = (s32[]{:T(128)}, bf16[2,512,512]{2,1,0:T(8,128)(2,1)}, f32[2,4,512]{2,1,0:T(4,128)S(1)}, bf16[2,1024,512]{1,2,0:T(8,128)(2,1)}, bf16[2,512,512]{1,2,...) while((s32[]{:T(128)}, bf16[2,512,512]{2,1,0:T(8,128)(2,1)}, f32[2,4,512]{2,1,0:T(4,128)S(1)}, ...), condition=%wide.region_6.7_spmd, body=%wide.region_3.0_spmd.sunk | while | flops 1092876288 | bytes 35717220 | solution.py:277
  177.2 20.6 %fusion.12 = (f32[1024,2048]{1,0:T(8,128)S(1)}, f32[1024,2048]{1,0:T(8,128)S(1)}) fusion(f32[2048]{0:T(1024)S(1)} %bitcast.388, bf16[512,2048]{0,1:T(8,128)(2,1)} %bitcast.373, f32[1024,512]{1,0:T(8,128)S(1)} %get-tuple-element.391, f32[512]{0:T(512)S(1)} %bitcast.401, f32[512]{0:T(512)S(1)} %bitcast.397, f32[1024]{0:T(1024)S(1)} %fusion.70, ...), kind=kOutput, calls=%fused_computation.34 | convolution fusion | flops 2282225664 | bytes 20992000 | tf_op jit(solution)/shard_map/dot_general | solution.py:282
  197.9 5.8 convert_reduce_fusion
  203.7 6.5 %multiply_reduce_fusion.2 = (f32[512]{0:T(512)}, f32[1024]{0:T(1024)S(1)}, f32[512]{0:T(512)}, f32[1024,512]{1,0:T(8,128)S(1)}) fusion(f32[1024,512]{1,0:T(8,128)S(1)} %get-tuple-element.391, f32[1024]{0:T(1024)S(1)} %fusion.70, f32[1024]{0:T(1024)S(1)} %broadcast_multiply_fusion.4, f32[512]{0:T(512)S(1)} %bitcast.398, ...), kind=kOutput, calls=%fused_computation.102 | convolution fusion | flops 2151675904 | bytes 10504192 | tf_op jit(solution)/shard_map/rf,df->rd/dot_general | solution.py:297
  215.5 36.3 %while.28 = (s32[]{:T(128)}, bf16[2,512,512]{2,1,0:T(8,128)(2,1)}, bf16[2,1024,512]{1,2,0:T(8,128)(2,1)}, bf16[2,1024,512]{1,2,0:T(8,128)(2,1)}, bf16[2,1024,512...) while((s32[]{:T(128)}, bf16[2,512,512]{2,1,0:T(8,128)(2,1)}, ...), condition=%wide.region_13.14_spmd, body=%wide.region_11.13_spmd.sunk | while | flops 2711091200 | bytes 84467848 | solution.py:305
  252.5 20.8 %fusion.15 = bf16[2048,1024]{0,1:T(8,128)(2,1)} fusion(f32[1024,2048]{1,0:T(8,128)} %copy-done.4, f32[2048]{0:T(1024)S(1)} %bitcast.390), kind=kLoop, calls=%fused_computation.37 | loop fusion | flops 138412032 | bytes 12591104 | tf_op jit(solution)/shard_map/convert_element_type | solution.py:286
  273.2 7.0 %copy.321 = bf16[2048,1024]{1,0:T(8,128)(2,1)} copy(bf16[2048,1024]{0,1:T(8,128)(2,1)} %fusion.15) | data formatting | bytes 8388608 | tf_op jit(solution)/shard_map/rf,rd->fd/dot_general | solution.py:291
  280.3 3.0 fusion.55
  283.3 6.8 %fusion.84 = f32[512,2048]{1,0:T(8,128)} fusion(bf16[1024,2048]{1,0:T(8,128)(2,1)} %copy-done.9, f32[1024,512]{1,0:T(8,128)S(1)} %copy-done.3, f32[512]{0:T(512)S(1)} %bitcast.402, f32[512]{0:T(512)S(1)} %bitcast.400, f32[1024]{0:T(1024)S(1)} %fusion.70, f32[1024]{0:T(1024)S(1)} %broadcast_multiply_fusion.4), kind=kOutput, calls=%fused_computation.190 | convolution fusion | flops 2150105088 | bytes 10498048 | tf_op jit(solution)/shard_map/rd,rf->df/dot_general | solution.py:295
  292.6 24.8 %reduce-scatter.7.cloned.1.call-done = bf16[2,256,512]{1,2,0:T(8,128)(2,1)} async-done(((bf16[2,1024,512]{1,2,0:T(8,128)(2,1)}), bf16[2,256,512]{1,2,0:T(8,128)(2,1)}) %reduce-scatter.7.cloned.1.call-update) | async-done | bytes 524304 | tf_op jit(solution)/shard_map/reduce_scatter | solution.py:319
  320.3 3.6 fusion.52
  326.5 4.4 convolution_dynamic-update-slice_fusion
  330.8 16.5 %copy.297 = f32[24,256,512]{2,0,1:T(8,128)} copy(f32[24,256,512]{2,1,0:T(8,128)} %bitcast.356) | data formatting | bytes 25165824 | tf_op jit(solution)/shard_map/reshape | solution.py:368
  351.8 10.8 %add_convert_fusion = bf16[1024,512]{1,0:T(8,128)(2,1)} fusion(f32[1024,512]{1,0:T(8,128)S(1)} %copy-done.3, bf16[2048,512]{1,0:T(8,128)(2,1)} %bitcast.360, f32[1024,2048]{1,0:T(8,128)} %copy-done.13, f32[1024,2048]{1,0:T(8,128)} %copy-done.4, f32[2048]{0:T(1024)S(1)} %bitcast.391, f32[512]{0:T(512)S(1)} %bitcast.413), kind=kOutput, calls=%fused_computation.109 | convolution fusion | flops 2157445120 | bytes 22030336 | tf_op jit(solution)/shard_map/dot_general | solution.py:288
  368.6 3.4 all-to-all-start.1
  372.3 9.1 %fusion = bf16[32,512]{1,0:T(8,128)(2,1)S(1)} fusion(bf16[100,512]{1,0:T(8,128)(2,1)S(1)} %fusion.60), kind=kCustom, calls=%all-reduce-scatter | all-reduce-scatter fusion | flops 65537 | bytes 135680
  382.9 42.8 %psum.23 = f32[10,512]{1,0:T(8,128)S(1)} all-reduce(f32[10,512]{1,0:T(8,128)S(1)} %concatenate.9), channel_id=1, replica_groups=mesh['feat'=4,'rows'=8] {'feat','rows'}, use_global_device_ids=true, to_apply=%region_29.30 | all-reduce | flops 5120 | bytes 40960 | tf_op jit(solution)/shard_map/psum | solution.py:366
  426.6 37.4 %psum.22 = f32[25,512]{1,0:T(8,128)S(1)} all-reduce(f32[25,512]{1,0:T(8,128)S(1)} %dynamic-slice_convert_fusion), channel_id=1, replica_groups=mesh['feat'=4,'rows'=8] {'rows'}, use_global_device_ids=true, to_apply=%region_21.22 | all-reduce | flops 12800 | bytes 102400 | tf_op jit(solution)/shard_map/psum | solution.py:367
  465.9 113.9 %all-reduce.4.cloned.1.call-done = f32[24,256,512]{2,0,1:T(8,128)} async-done(((f32[24,256,512]{2,0,1:T(8,128)}), f32[24,256,512]{2,0,1:T(8,128)}) %all-reduce.4.cloned.1.call-update) | async-done | bytes 12582928 | tf_op jit(solution)/shard_map/psum | solution.py:366
  579.7 7.4 %fusion.72 = f32[4,256,512]{2,0,1:T(4,128)S(1)} fusion(f32[24,256,512]{2,0,1:T(8,128)} %all-reduce.4.cloned.1.call-done, s32[24]{0:T(128)S(1)} %copy-done.58, pred[24]{0:T(512)(128)(4,1)S(1)} %copy-done.59), kind=kOutput, calls=%fused_computation.177 | convolution fusion | flops 150995136 | bytes 14680184 | tf_op jit(solution)/shard_map/ci,ixy->cxy/dot_general | solution.py:369
  587.2 6.3 %fusion.91 = (bf16[4,256,512]{2,1,0:T(8,128)(2,1)}, f32[4,256,512]{2,1,0:T(8,128)}, f32[4,256,512]{2,1,0:T(8,128)}, f32[4,256,512]{2,1,0:T(8,128)}, f32[4,256,512]{2,1,0:T(8,128)}) fusion(f32[4]{0:T(128)S(1)} %convert_reduce_fusion.3, f32[4,256,512]{2,1,0:T(8,128)S(1)} %copy-done.12, f32[4,256,512]{2,1,0:T(8,128)S(1)} %copy-done.19, ...), kind=kLoop, calls=%fused_computation.194 | loop fusion | flops 10485760 | bytes 17825808 | tf_op jit(solution)/shard_map/convert_element_type | solution.py:388
  (257 shorter events, 117.0 us)
Async XLA Ops:
  13.2 81.7 %all-to-all-start = ((bf16[4,2,12800]{2,1,0:T(2,128)(2,1)}), bf16[4,2,12800]{2,1,0:T(2,128)(2,1)S(1)}, u32[]{:S(2)}, u32[]{:S(2)}) async-start(bf16[4,2,12800]{2,1,0:T(2,128)(2,1)} %reshape.466), calls=%async_computation | async-start | bytes 409600 | tf_op jit(solution)/shard_map/all_to_all | solution.py:252
  17.4 108.2 %all-gather.6.cloned.1.call-start = ((), (), s32[]{:S(2)}) async-start(), calls=%async_computation.5 | async-start | bytes 2621440 | tf_op jit(solution)/shard_map/all_gather | solution.py:273
  26.1 72.8 %copy-start.27 = (bf16[100,512,1,1]{1,0,2,3:T(8,128)(2,1)}, bf16[100,512,1,1]{1,0,2,3:T(8,128)(2,1)S(1)}, u32[]{:S(2)}) copy-start(bf16[100,512,1,1]{1,0,2,3:T(8,128)(2,1)S(1)} %reshape.455) | copy-start | bytes 307204
  94.9 16.5 %copy-start.40 = (f32[1,512]{1,0:T(1,128)}, f32[1,512]{1,0:T(1,128)S(1)}, u32[]{:S(2)}) copy-start(f32[1,512]{1,0:T(1,128)S(1)} %get-tuple-element.379) | copy-start | bytes 6148
  94.9 82.3 %copy-start.50 = (f32[1,512]{1,0:T(1,128)}, f32[1,512]{1,0:T(1,128)S(1)}, u32[]{:S(2)}) copy-start(f32[1,512]{1,0:T(1,128)S(1)} %get-tuple-element.376) | copy-start | bytes 6148
  99.5 75.1 %copy-start = (f32[2,2,256,512]{3,2,1,0:T(8,128)}, f32[2,2,256,512]{3,2,1,0:T(8,128)S(1)}, u32[]{:S(2)}) copy-start(f32[2,2,256,512]{3,2,1,0:T(8,128)S(1)} %get-tuple-element.389) | copy-start | bytes 6291460
  100.6 15.0 %copy-start.44 = (f32[2,2,256]{2,1,0:T(2,128)}, f32[2,2,256]{2,1,0:T(2,128)S(1)}, u32[]{:S(2)}) copy-start(f32[2,2,256]{2,1,0:T(2,128)S(1)} %fusion.81) | copy-start | bytes 12292
  101.2 14.4 %copy-start.17 = (bf16[2,2,256,512]{3,2,1,0:T(8,128)(2,1)}, bf16[2,2,256,512]{3,2,1,0:T(8,128)(2,1)S(1)}, u32[]{:S(2)}) copy-start(bf16[2,2,256,512]{3,2,1,0:T(8,128)(2,1)S(1)} %add_convert_fusion.2) | copy-start | bytes 3145732
  103.8 46.5 %all-gather.4.cloned.1.call-start = ((), (), s32[]{:S(2)}) async-start(), calls=%async_computation.4 | async-start | bytes 2621440 | tf_op jit(solution)/shard_map/all_gather | solution.py:274
  106.2 183.9 %reduce-scatter.5.cloned.1.call-start = ((), (), s32[]{:S(2)}) async-start(), calls=%async_computation.6 | async-start | bytes 2621440 | tf_op jit(solution)/shard_map/reduce_scatter | solution.py:316
  176.7 33.5 %copy-start.2 = (f32[1024,512]{1,0:T(8,128)}, f32[1024,512]{1,0:T(8,128)S(1)}, u32[]{:S(2)}) copy-start(f32[1024,512]{1,0:T(8,128)S(1)} %get-tuple-element.391) | copy-start | bytes 6291460
  177.2 20.7 %copy-start.10 = (bf16[2,2,256,512]{3,2,1,0:T(8,128)(2,1)S(1)}, bf16[2,2,256,512]{3,2,1,0:T(8,128)(2,1)}, u32[]{:S(2)}) copy-start(bf16[2,2,256,512]{3,2,1,0:T(8,128)(2,1)} %param.24) | copy-start | bytes 3145732
  177.2 20.7 %copy-start.14 = (bf16[8,256,512]{2,1,0:T(8,128)(2,1)S(1)}, bf16[8,256,512]{2,1,0:T(8,128)(2,1)}, u32[]{:S(2)}) copy-start(bf16[8,256,512]{2,1,0:T(8,128)(2,1)} %get-tuple-element.367) | copy-start | bytes 6291460
  251.8 65.6 %reduce-scatter.7.cloned.1.call-start = ((), (), s32[]{:S(2)}) async-start(), calls=%async_computation.7 | async-start | bytes 2621440 | tf_op jit(solution)/shard_map/reduce_scatter | solution.py:319
  252.4 27.9 %copy-start.15 = (bf16[2,512,512]{2,1,0:T(8,128)(2,1)S(1)}, bf16[2,512,512]{2,1,0:T(8,128)(2,1)}, u32[]{:S(2)}) copy-start(bf16[2,512,512]{2,1,0:T(8,128)(2,1)} %get-tuple-element.112) | copy-start | bytes 3145732
  252.4 327.3 %all-reduce.4.cloned.1.call-start = ((), (), s32[]{:S(2)}) async-start(), calls=%async_computation.8 | async-start | bytes 25165824 | tf_op jit(solution)/shard_map/psum | solution.py:366
  292.6 33.9 %copy-start.11 = (bf16[2,2,256,512]{3,2,1,0:T(8,128)(2,1)S(1)}, bf16[2,2,256,512]{3,2,1,0:T(8,128)(2,1)}, u32[]{:S(2)}) copy-start(bf16[2,2,256,512]{3,2,1,0:T(8,128)(2,1)} %param.24) | copy-start | bytes 3145732
  351.8 11.9 %copy-start.1 = (f32[2,2,256,512]{3,2,1,0:T(8,128)S(1)}, f32[2,2,256,512]{3,2,1,0:T(8,128)}, u32[]{:S(2)}) copy-start(f32[2,2,256,512]{3,2,1,0:T(8,128)} %copy-done) | copy-start | bytes 6291460
  364.3 18.4 %copy-start.60 = (f32[512]{0:T(512)S(1)}, f32[512]{0:T(512)}, u32[]{:S(2)}) copy-start(f32[512]{0:T(512)} %get-tuple-element.309) | copy-start | bytes 6148
  364.4 18.4 %copy-start.61 = (f32[512]{0:T(512)S(1)}, f32[512]{0:T(512)}, u32[]{:S(2)}) copy-start(f32[512]{0:T(512)} %get-tuple-element.311) | copy-start | bytes 6148
  364.4 61.2 %copy-start.37 = (f32[10,512]{1,0:T(8,128)S(1)}, f32[10,512]{1,0:T(8,128)}, u32[]{:S(2)}) copy-start(f32[10,512]{1,0:T(8,128)} %param.31) | copy-start | bytes 61444
  364.4 61.2 %copy-start.48 = (f32[10,512]{1,0:T(8,128)S(1)}, f32[10,512]{1,0:T(8,128)}, u32[]{:S(2)}) copy-start(f32[10,512]{1,0:T(8,128)} %param.33) | copy-start | bytes 61444
  364.5 61.2 %copy-start.49 = (f32[10,512]{1,0:T(8,128)S(1)}, f32[10,512]{1,0:T(8,128)}, u32[]{:S(2)}) copy-start(f32[10,512]{1,0:T(8,128)} %param.32) | copy-start | bytes 61444
  364.5 99.5 %copy-start.31 = (f32[25,512]{1,0:T(8,128)S(1)}, f32[25,512]{1,0:T(8,128)}, u32[]{:S(2)}) copy-start(f32[25,512]{1,0:T(8,128)} %param.28) | copy-start | bytes 153604
  364.5 99.5 %copy-start.38 = (f32[25,512]{1,0:T(8,128)S(1)}, f32[25,512]{1,0:T(8,128)}, u32[]{:S(2)}) copy-start(f32[25,512]{1,0:T(8,128)} %param.30) | copy-start | bytes 153604
  364.5 99.5 %copy-start.39 = (f32[25,512]{1,0:T(8,128)S(1)}, f32[25,512]{1,0:T(8,128)}, u32[]{:S(2)}) copy-start(f32[25,512]{1,0:T(8,128)} %param.29) | copy-start | bytes 153604
  364.5 100.4 %copy-start.56 = (bf16[2,25]{1,0:T(2,128)(2,1)S(1)}, bf16[2,25]{1,0:T(2,128)(2,1)}, u32[]{:S(2)}) copy-start(bf16[2,25]{1,0:T(2,128)(2,1)} %copy-done.55) | copy-start | bytes 304
  368.6 96.2 %all-to-all-start.1 = ((bf16[2,2,256,100]{2,1,0,3:T(2,128)(2,1)}), bf16[2,2,256,100]{2,1,0,3:T(2,128)(2,1)S(1)}, u32[]{:S(2)}, u32[]{:S(2)}) async-start(bf16[2,2,256,100]{2,1,0,3:T(2,128)(2,1)} %copy.287), calls=%async_computation.3 | async-start | bytes 409600 | tf_op jit(solution)/shard_map/all_to_all | solution.py:349
  381.4 45.0 %collective-permute-start = (bf16[21,512]{1,0:T(8,128)(2,1)S(1)}, bf16[21,512]{1,0:T(8,128)(2,1)S(1)}, u32[]{:S(2)}, u32[]{:S(2)}) collective-permute-start(bf16[21,512]{1,0:T(8,128)(2,1)S(1)} %slice.103), channel_id=1, source_target_pairs={{0,8},{8,16},{16,24},{1,9},{9,17},{17,25},{2,10},{10,18},{18,26},{... | collective-permute-start | bytes 64520
  425.7 161.4 %copy-start.33 = (f32[10,512]{1,0:T(8,128)}, f32[10,512]{1,0:T(8,128)S(1)}, u32[]{:S(2)}) copy-start(f32[10,512]{1,0:T(8,128)S(1)} %psum.23) | copy-start | bytes 61444
  426.4 160.8 %copy-start.12 = (f32[4,256,512]{2,1,0:T(8,128)S(1)}, f32[4,256,512]{2,1,0:T(8,128)}, u32[]{:S(2)}) copy-start(f32[4,256,512]{2,1,0:T(8,128)} %slots_ref.1) | copy-start | bytes 6291460
  464.0 129.5 %copy-start.32 = (f32[25,512]{1,0:T(8,128)}, f32[25,512]{1,0:T(8,128)S(1)}, u32[]{:S(2)}) copy-start(f32[25,512]{1,0:T(8,128)S(1)} %psum.22) | copy-start | bytes 153604
  (39 other events, 206.8 us)
Sparse Core Ops, SparseCore 0:
  104.0 21.5 all-gather.5
  127.7 22.5 all-gather.3
  252.0 31.4 reduce-scatter.4
  286.0 31.4 reduce-scatter.6
  347.6 232.1 all-reduce.3

commit v2 on v0

v2 whole, which is shorter than its diff:
```python
import functools
import math

import jax
import jax.numpy as jnp
from jax import lax
from jax.experimental import pallas as pl
from jax.experimental.pallas import tpu as pltpu
from jax.sharding import PartitionSpec as P

MESH = pl.DeviceIdType.MESH
bf16, f32 = jnp.bfloat16, jnp.float32
NN = (((1,), (0,)), ((), ()))
NT = (((1,), (1,)), ((), ()))
TN = (((0,), (0,)), ((), ()))
LOG2E = math.log2(math.e)
HEADS = 4
HEAD_DIM = 128
STEP = 10
LN_EPS = 1e-05
BETA_FIRST = 0.9
BETA_SECOND = 0.999
ADAM_EPS = 1e-08
DECAY = 0.01
RATE_MATRIX = 0.1
RATE_EMBED = 0.3
RATE_SMALL = 0.6
D = 512
HALF = 1024
QUART = 256
PADF = 32
VMEM_BYTES = 60 * 2**20


def dot(a, b, dims=NN):
    return lax.dot_general(a, b, dims, preferred_element_type=f32)


def vmem():
    return pl.BlockSpec(memory_space=pltpu.VMEM)


def anyspace():
    return pl.BlockSpec(memory_space=pl.ANY)


def smem():
    return pl.BlockSpec(memory_space=pltpu.SMEM)


def remote(src, dst, send, recv, dev):
    return pltpu.make_async_remote_copy(
        src_ref=src, dst_ref=dst, send_sem=send, recv_sem=recv, device_id=dev, device_id_type=MESH
    )


def greet(peers):
    bar = pltpu.get_barrier_semaphore()
    for d in peers:
        pl.semaphore_signal(bar, inc=1, device_id=d, device_id_type=MESH)
    return bar


GROUPS = ((1, 3, True), (0, 1, False))


def gather_kernel(
    R, slots_ref, feat_ref, mask_ref, tmap_ref, emb_ref, small_ref,
    G_ref, XT_ref, h0_ref, a1s_ref, a1q_ref, n1s_ref, n1q_ref, rs_ref, rq_ref,
    own, XTo, XTa, tmpq, lsem, fs, fr, hs, hr, xs, xr, cs, cr, c2s, c2r,
):
    f = lax.axis_index("feat")
    r = lax.axis_index("rows")
    x = f // 2
    c = f % 2
    n = R.bit_length() - 1
    S, BR, W = own.shape
    BH, CH = BR // 2, W // 2
    core_id = (f ^ 1, r)
    x_id = (f ^ 2, r)
    row_id = [(f, r ^ (1 << (n - 1 - j))) for j in range(n)]
    peers = [core_id, x_id] + row_id
    bar = greet(peers)
    own[...] = slots_ref[...].astype(bf16)
    pl.semaphore_wait(bar, len(peers))
    local = pltpu.make_async_copy(own, G_ref.at[0], lsem)
    local.start()
    subs = [(j, g) for j in range(n) for g in range(-1, j)]
    index = {jg: i for i, jg in enumerate(subs)}

    def span(g):
        return (0, 1) if g < 0 else (1 << g, 1 << g)

    def region(s, half_col):
        rows = pl.ds(pl.multiple_of(c * BH, BH), BH)
        cols = pl.ds(pl.multiple_of(half_col * CH, CH), CH) if GROUPS[s][2] else pl.ds(0, W)
        return pl.ds(GROUPS[s][0], GROUPS[s][1]), rows, cols

    def hyper(s, j, g):
        where = region(s, x)
        start, size = span(g)
        k = index[(j, g)]
        if g < 0:
            src, dst = own.at[where], G_ref.at[(1 << j, *where)]
        else:
            src = G_ref.at[(pl.ds(start, size), *where)]
            dst = G_ref.at[(pl.ds((1 << j) + start, size), *where)]
        return remote(src, dst, hs.at[s, k], hr.at[s, k], row_id[j])

    def forward(s, j, g, half_col, sems, semr, dev):
        start, size = span(g)
        k = index[(j, g)]
        ref = G_ref.at[(pl.ds((1 << j) + start, size), *region(s, half_col))]
        return remote(ref, ref, sems.at[s, k], semr.at[s, k], dev)

    order = range(len(GROUPS))
    for s in order:
        for j in range(n):
            hyper(s, j, -1).start()

    T = mask_ref.shape[0]
    nf = feat_ref.shape[3]
    row_iota = lax.broadcasted_iota(jnp.int32, (T, nf), 0)
    for t in range(2):
        line = jnp.sum(jnp.where(row_iota == tmap_ref[t], mask_ref[...], 0), axis=0, keepdims=True)
        diag = jnp.where(
            lax.broadcasted_iota(jnp.int32, (PADF, nf), 0) == lax.broadcasted_iota(jnp.int32, (PADF, nf), 1),
            jnp.broadcast_to(line, (PADF, nf)), 0,
        ).astype(f32).astype(bf16)
        XTo[:, pl.ds(t * HALF, HALF)] = dot(diag, feat_ref[t, 0], NT).astype(bf16)
        query = dot(diag, feat_ref[t, 1], NT).astype(bf16)
        for k in range(4):
            XTo[:, pl.ds(2 * HALF + D + k * 512 + t * QUART, QUART)] = query[:, k * QUART:(k + 1) * QUART]
    XTo[:, pl.ds(2 * HALF, D)] = jnp.zeros((PADF, D), bf16)
    XTo[pl.ds(0, nf), pl.ds(2 * HALF, D)] = emb_ref[...].astype(bf16)
    wide = 2 * HALF + D
    shared = pl.ds(0, wide)

    def rows_of(dev):
        return pl.ds(pl.multiple_of(dev * PADF, PADF), PADF)

    def chunk_of(dev):
        return pl.ds(pl.multiple_of(wide + dev * 512, 512), 512)

    tail = pl.ds(wide, 512)
    feats = [
        remote(XTo.at[:, shared], XTa.at[rows_of(f), shared], fs.at[0], fr.at[0], core_id),
        remote(XTo.at[:, chunk_of(f ^ 1)], XTa.at[rows_of(f), tail], fs.at[1], fr.at[1], core_id),
        remote(XTo.at[:, shared], XTa.at[rows_of(f), shared], fs.at[2], fr.at[2], x_id),
        remote(XTo.at[:, chunk_of(f ^ 2)], XTa.at[rows_of(f), tail], fs.at[3], fr.at[3], x_id),
        remote(XTo.at[:, chunk_of(f ^ 3)], tmpq, fs.at[4], fr.at[4], x_id),
        remote(XTa.at[rows_of(f ^ 2), shared], XTa.at[rows_of(f ^ 2), shared], fs.at[5], fr.at[5], core_id),
        remote(tmpq, XTa.at[rows_of(f ^ 2), tail], fs.at[6], fr.at[6], core_id),
    ]
    for copy in feats[:5]:
        copy.start()
    XTa[rows_of(f), shared] = XTo[:, shared]
    XTa[rows_of(f), tail] = XTo[:, chunk_of(f)]

    def x_arrive(j):
        for s in order:
            if GROUPS[s][2]:
                for g in range(-1, j):
                    forward(s, j, g, x, xs, xr, x_id).wait_recv()
                    forward(s, j, g, 1 - x, c2s, c2r, core_id).start()

    def hyper_arrive(j):
        for s in order:
            for g in range(-1, j):
                hyper(s, j, g).wait_recv()
                if GROUPS[s][2]:
                    forward(s, j, g, x, xs, xr, x_id).start()
                forward(s, j, g, x, cs, cr, core_id).start()
            for j2 in range(j + 1, n):
                hyper(s, j2, j).start()

    hyper_arrive(0)
    feats[2].wait_recv()
    feats[4].wait_recv()
    feats[5].start()
    feats[6].start()
    for j in range(1, n - 1):
        hyper_arrive(j)
        x_arrive(j - 1)
    for k in (0, 1, 3, 5, 6):
        feats[k].wait_recv()

    shift0 = small_ref[0:1]
    gain = small_ref[1:2]
    shift = small_ref[2:3]
    E = XTa[:, pl.ds(2 * HALF, D)]

    def norm(cols):
        h = dot(XTa[:, cols], E, TN) + shift0
        mean = jnp.mean(h, axis=-1, keepdims=True)
        cen = h - mean
        rstd = lax.rsqrt(jnp.mean(cen * cen, axis=-1, keepdims=True) + LN_EPS)
        nrm = cen * rstd
        return h, nrm, rstd, (nrm * gain + shift).astype(bf16)

    @pl.loop(0, 8)
    def _(i):
        rows = pl.ds(pl.multiple_of(i * QUART, QUART), QUART)
        h, nrm, rstd, act = norm(rows)
        n1s_ref[rows] = nrm.astype(bf16)
        a1s_ref[rows] = act
        rs_ref[rows] = jnp.broadcast_to(rstd, (QUART, 128))

        @pl.when(i % 4 == f)
        def _():
            h0_ref[pl.ds(pl.multiple_of((i // 4) * 512, 512), QUART)] = h

    @pl.loop(0, 2)
    def _(t):
        rows = pl.ds(pl.multiple_of(t * QUART, QUART), QUART)
        h, nrm, rstd, act = norm(pl.ds(pl.multiple_of(wide + t * QUART, QUART), QUART))
        n1q_ref[rows] = nrm.astype(bf16)
        a1q_ref[rows] = act
        rq_ref[rows] = jnp.broadcast_to(rstd, (QUART, 128))
        h0_ref[pl.ds(pl.multiple_of(t * 512 + QUART, QUART), QUART)] = h

    XT_ref[...] = XTa[...]
    hyper_arrive(n - 1)
    if n > 1:
        x_arrive(n - 2)
    x_arrive(n - 1)
    local.wait()
    for copy in feats:
        copy.wait_send()
    for s in order:
        for j, g in subs:
            hyper(s, j, g).wait_send()
            forward(s, j, g, x, cs, cr, core_id).wait()
            if GROUPS[s][2]:
                forward(s, j, g, x, xs, xr, x_id).wait_send()
                forward(s, j, g, 1 - x, c2s, c2r, core_id).wait()


def gather_call(R, slots, features, masks, tmap, emb, small):
    S, BR, W = slots.shape
    n = R.bit_length() - 1
    M = n * (n + 1) // 2
    sem = pltpu.SemaphoreType.DMA((len(GROUPS), M))
    sd = jax.ShapeDtypeStruct
    cols = 2 * HALF + D + 512
    return pl.pallas_call(
        functools.partial(gather_kernel, R),
        out_shape=(
            sd((R, S, BR, W), bf16), sd((4 * PADF, cols), bf16), sd((1024, D), f32),
            sd((2048, D), bf16), sd((512, D), bf16), sd((2048, D), bf16), sd((512, D), bf16),
            sd((2048, 128), f32), sd((512, 128), f32),
        ),
        in_specs=[vmem(), vmem(), vmem(), smem(), vmem(), vmem()],
        out_specs=(anyspace(),) + (vmem(),) * 8,
        scratch_shapes=[
            pltpu.VMEM((S, BR, W), bf16), pltpu.VMEM((PADF, 2 * HALF + D + 2048), bf16),
            pltpu.VMEM((4 * PADF, cols), bf16), pltpu.VMEM((PADF, 512), bf16),
            pltpu.SemaphoreType.DMA, pltpu.SemaphoreType.DMA((7,)), pltpu.SemaphoreType.DMA((7,)),
        ] + [sem] * 8,
        compiler_params=pltpu.CompilerParams(collective_id=0, has_side_effects=True, vmem_limit_bytes=VMEM_BYTES),
        name="gather_weights",
    )(slots, features, masks, tmap, emb, small)


def gelu_pair(u):
    t = 1.0 / (1.0 + (0.3275911 * math.sqrt(0.5)) * jnp.abs(u))
    ex = jnp.exp2((-0.5 * LOG2E) * (u * u))
    poly = t * (0.127414796 + t * (-0.142248368 + t * (0.7107068705 + t * (-0.7265760135 + t * 0.5307027145))))
    e = poly * ex
    phi = jnp.where(u >= 0, 1.0 - e, e)
    return u * phi, phi + u * ex * (1.0 / math.sqrt(2 * math.pi))


def forward_kernel(
    BR, pos, G, h0o, a1s, a1q, dY, small,
    out, gF, dy1, sg, ET, linv, OT, qo, ko, kTo, vo, Wout,
    W, q_s, k_s, kT_s, v_s, vT_s, ET_s, OT_s, O_s, a2_s, G_s, dU_s, gF_s, wsem, osem,
):
    U = W.shape[0] // BR
    R = U // 3
    f = lax.axis_index("feat")
    per = D // BR
    BH = BR // 2

    def wcopy(u):
        return pltpu.make_async_copy(G.at[pos[u]], W.at[pl.ds(u * BR, BR)], wsem.at[u])

    for u in range(U):
        wcopy(u).start()

    def wwait(i):
        for u in range(i * per, (i + 1) * per):
            wcopy(u).wait()

    def mat(i):
        return W[pl.ds(i * D, D)]

    scale = (HEAD_DIM**-0.5) * LOG2E
    outs = []

    def ship(src, dst):
        copy = pltpu.make_async_copy(src, dst, osem.at[len(outs)])
        copy.start()
        outs.append(copy)

    wwait(0)
    for t in range(2):
        sup = pl.multiple_of(t * HALF + f * QUART, QUART)
        q_s[pl.ds(t * 512, QUART)] = (dot(a1s[pl.ds(sup, QUART)], mat(0)) * scale).astype(bf16)
        q_s[pl.ds(t * 512 + QUART, QUART)] = (dot(a1q[pl.ds(t * QUART, QUART)], mat(0)) * scale).astype(bf16)
    wwait(1)
    wwait(2)

    @pl.loop(0, 4)
    def _(i):
        rows = pl.ds(pl.multiple_of(i * 512, 512), 512)
        a = a1s[rows]
        k = dot(a, mat(1)).astype(bf16)
        k_s[rows] = k
        kT_s[:, rows] = k.T
        v = dot(a, mat(2)).astype(bf16)
        v_s[rows] = v
        vT_s[:, rows] = v.T

    @pl.loop(0, 8)
    def _(i):
        t = i // HEADS
        h = i % HEADS
        ks = pl.ds(pl.multiple_of(t * HALF, HALF), HALF)
        qs = pl.ds(pl.multiple_of(t * 512, 512), 512)
        hs = pl.ds(pl.multiple_of(h * HEAD_DIM, HEAD_DIM), HEAD_DIM)
        st = dot(k_s[ks, hs], q_s[qs, hs], NT)
        top = jnp.max(st, axis=0, keepdims=True)
        e = jnp.exp2(st - top)
        inv = 1.0 / jnp.sum(e, axis=0, keepdims=True)
        eb = e.astype(bf16)
        ET_s[i] = eb
        linv[pl.ds(i, 1)] = inv
        ot = (dot(vT_s[hs, ks], eb) * inv).astype(bf16)
        OT_s[hs, qs] = ot
        O_s[qs, hs] = ot.T

    wwait(3)
    ship(q_s, qo)
    ship(k_s, ko)
    ship(kT_s, kTo)
    ship(v_s, vo)
    ship(ET_s, ET)
    ship(OT_s, OT)
    ship(W.at[pl.ds(0, 4 * D)], Wout)
    for i in range(4, 12):
        wwait(i)
    gain = small[3:4]
    shift = small[4:5]
    sg[...] = jnp.zeros_like(sg)
    RB = 256

    @pl.loop(0, 1024 // RB)
    def _(i):
        rows = pl.ds(pl.multiple_of(i * RB, RB), RB)
        y1 = h0o[rows] + dot(O_s[rows], mat(3))
        mean = jnp.mean(y1, axis=-1, keepdims=True)
        cen = y1 - mean
        rstd = lax.rsqrt(jnp.mean(cen * cen, axis=-1, keepdims=True) + LN_EPS)
        n2 = cen * rstd
        a2 = (n2 * gain + shift).astype(bf16)
        a2_s[rows] = a2
        dy = dY[rows]
        acc = y1 + small[5:6]
        da2 = jnp.zeros((RB, D), f32)
        for j in range(4):
            cols = pl.ds(j * 512, 512)
            wu = mat(4 + j)
            wd = mat(8 + j)
            u = dot(a2, wu) + small[6 + j:7 + j]
            gl, gp = gelu_pair(u)
            gb = gl.astype(bf16)
            G_s[rows, cols] = gb
            acc = acc + dot(gb, wd)
            du = (dot(dy, wd, NT) * gp).astype(bf16)
            dU_s[rows, cols] = du
            sg[6 + j:7 + j] += jnp.sum(du.astype(f32), axis=0, keepdims=True)
            da2 = da2 + dot(du, wu, NT)
        out[rows] = acc.astype(bf16)
        dyf = dy.astype(f32)
        sg[3:4] += jnp.sum(da2 * n2, axis=0, keepdims=True)
        sg[4:5] += jnp.sum(da2, axis=0, keepdims=True)
        sg[5:6] += jnp.sum(dyf, axis=0, keepdims=True)
        cc = da2 * gain
        m1 = jnp.mean(cc, axis=-1, keepdims=True)
        m2 = jnp.mean(cc * n2, axis=-1, keepdims=True)
        dy1[rows] = dyf + rstd * (cc - m1 - n2 * m2)

    def put(chunk, j, val):
        for m in range(2):
            for c in range(2):
                k = 2 * m + c
                gF_s[chunk * 2 + m, c, pl.ds(j * per, per)] = val[:, k * 128:(k + 1) * 128].reshape(per, 2, BH, 128)

    for j in range(4):
        put(1, j, dot(G_s[:, pl.ds(j * 512, 512)], dY[...], TN).astype(bf16))
    for j in range(4):
        put(0, j, dot(a2_s[...], dU_s[:, pl.ds(j * 512, 512)], TN).astype(bf16))
    ship(gF_s, gF)
    for copy in outs:
        copy.wait()


def forward_call(pos, G, h0o, a1s, a1q, dY, small):
    BR = G.shape[1]
    U = pos.shape[0]
    R = U // 3
    sd = jax.ShapeDtypeStruct
    gshape = (4, 2, R, 2, BR // 2, 128)
    V = pltpu.VMEM
    return pl.pallas_call(
        functools.partial(forward_kernel, BR),
        out_shape=(
            sd((1024, D), bf16), sd(gshape, bf16), sd((1024, D), f32), sd((16, D), f32),
            sd((8, HALF, 512), bf16), sd((8, 512), f32), sd((D, 1024), bf16), sd((1024, D), bf16),
            sd((2048, D), bf16), sd((D, 2048), bf16), sd((2048, D), bf16), sd((2048, D), bf16),
        ),
        in_specs=[smem(), anyspace()] + [vmem()] * 5,
        out_specs=(vmem(), anyspace(), vmem(), vmem(), anyspace(), vmem()) + (anyspace(),) * 6,
        scratch_shapes=[
            V((U * BR, D), bf16), V((1024, D), bf16), V((2048, D), bf16), V((D, 2048), bf16), V((2048, D), bf16),
            V((D, 2048), bf16), V((8, HALF, 512), bf16), V((D, 1024), bf16), V((1024, D), bf16), V((1024, D), bf16),
            V((1024, 2048), bf16), V((1024, 2048), bf16), V(gshape, bf16),
            pltpu.SemaphoreType.DMA((U,)), pltpu.SemaphoreType.DMA((8,)),
        ],
        compiler_params=pltpu.CompilerParams(vmem_limit_bytes=VMEM_BYTES),
        name="forward",
    )(pos, G, h0o, a1s, a1q, dY, small)


CHUNKS = ((2, 2), (0, 2), (4, 1), (5, 1))


def backward_kernel(
    R, gF, su, occ, dy1, W4, ET, linv, OT, qs, ks, kT, vs, a1s, a1q, n1s, n1q, rs, rq, XT, small, sgF,
    FIN, SM, EM, GI,
    ETb, dZ, dOT, Dp, dq, dk, dv, sg, eg, GT,
    gA, ownF, RC, S1, RX, S2, RH, AGB, SEL, PK, RK, GC, XS, XR,
    esem, osem, ss, sr, fs, fr, ps, pr, gs, gr,
):
    f = lax.axis_index("feat")
    r = lax.axis_index("rows")
    x = f // 2
    c = f % 2
    n = R.bit_length() - 1
    BH = gA.shape[4]
    per = D // (2 * BH)
    core_id = (f ^ 1, r)
    x_id = (f ^ 2, r)
    row_id = [(f, r ^ (1 << j)) for j in range(n)]
    peers = [core_id, x_id] + row_id
    bar = greet(peers)

    def ecopy(i):
        return pltpu.make_async_copy(ET.at[i], ETb.at[i], esem.at[i])

    order = [t * HEADS + h for h in range(HEADS) for t in range(2)]
    ownc = pltpu.make_async_copy(gF.at[:, c], ownF, osem)
    ownc.start()
    for i in order:
        ecopy(i).start()
    pl.semaphore_wait(bar, len(peers))

    bits = [(r >> j) & 1 for j in range(n)]
    base = [0]
    for j in range(n):
        base.append(base[j] + bits[j] * (R >> (j + 1)))

    def groups(k):
        return pl.ds(CHUNKS[k][0], CHUNKS[k][1])

    def core_copy(k):
        g0, ng = CHUNKS[k]
        src = gF.at[groups(k), 1 - c] if g0 < 4 else gA.at[pl.ds(g0 - 4, ng), 1 - c]
        return remote(src, RC.at[groups(k)], ss.at[k, 0], sr.at[k, 0], core_id)

    def x_copy(k):
        return remote(S1.at[1 - x, groups(k)], RX.at[groups(k)], ss.at[k, 1], sr.at[k, 1], x_id)

    def rs_copy(k, j):
        half = R >> (j + 1)
        away = base[j] + (1 - bits[j]) * half
        off = R - (R >> j)
        return remote(
            S2.at[groups(k), pl.ds(away, half)], RH.at[groups(k), pl.ds(off, half)],
            ss.at[k, 2 + j], sr.at[k, 2 + j], row_id[j],
        )

    def ag_copy(k, j):
        size = R >> (j + 1)
        ref = AGB.at[groups(k), pl.ds(base[j + 1], size)]
        return remote(ref, ref, ss.at[k, 2 + n + j], sr.at[k, 2 + n + j], row_id[j])

    def step(k, stage):
        g0, ng = CHUNKS[k]
        gl = range(g0, g0 + ng)
        if stage == 0:
            core_copy(k).wait_recv()
            for g in gl:
                for p in range(R):
                    for h in range(2):
                        mine = ownF[g, p, h] if g < 4 else gA[g - 4, c, p, h]
                        S1[h, g, p] = (mine.astype(f32) + RC[g, p, h].astype(f32)).astype(bf16)
            x_copy(k).start()
        elif stage == 1:
            x_copy(k).wait_recv()
            for g in gl:
                S2[g] = (S1[x, g].astype(f32) + RX[g].astype(f32)).astype(bf16)
            rs_copy(k, 0).start()
        elif stage < 2 + n:
            j = stage - 2
            half = R >> (j + 1)
            off = R - (R >> j)
            rs_copy(k, j).wait_recv()
            keep = pl.ds(base[j + 1], half)
            for g in gl:
                total = (S2[g, keep].astype(f32) + RH[g, pl.ds(off, half)].astype(f32)).astype(bf16)
                if j < n - 1:
                    S2[g, keep] = total
                else:
                    AGB[g, keep] = total
            if j < n - 1:
                rs_copy(k, j + 1).start()
            else:
                ag_copy(k, n - 1).start()
        else:
            j = 2 * n + 1 - stage
            ag_copy(k, j).wait_recv()
            if j > 0:
                ag_copy(k, j - 1).start()

    core_copy(0).start()
    core_copy(1).start()

    scale = HEAD_DIM**-0.5
    for i in range(2):
        dZ[pl.ds(i * 512, 512)] = dy1[pl.ds(i * 512, 512)].astype(bf16)

    def put(m, i, val):
        for cc in range(2):
            gA[m, cc, pl.ds(i * per, per)] = val[:, cc * 128:(cc + 1) * 128].reshape(per, 2, BH, 128)

    go = dot(OT[...], dZ[...]).astype(bf16)
    put(0, 3, go[:, :256])
    put(1, 3, go[:, 256:])
    for t in range(2):
        cols = pl.ds(t * 512, 512)
        for h in range(HEADS):
            rows = pl.ds(h * HEAD_DIM, HEAD_DIM)
            d = dot(W4[pl.ds(3 * D + h * HEAD_DIM, HEAD_DIM)], dZ[cols], NT) * linv[pl.ds(t * HEADS + h, 1)]
            Dp[pl.ds(t * HEADS + h, 1)] = jnp.sum(d * OT[rows, cols].astype(f32), axis=0, keepdims=True)
            dOT[rows, cols] = d.astype(bf16)
    ownc.wait()
    step(0, 0)
    step(1, 0)

    def heads(h):
        hs = pl.ds(h * HEAD_DIM, HEAD_DIM)
        for t in range(2):
            ecopy(t * HEADS + h).wait()

        @pl.loop(0, 2)
        def _(t):
            i = t * HEADS + h
            ksl = pl.ds(pl.multiple_of(t * HALF, HALF), HALF)
            qsl = pl.ds(pl.multiple_of(t * 512, 512), 512)
            do = dOT[hs, qsl]
            dp = dot(vs[ksl, hs], do)
            e = ETb[i]
            ds = (e.astype(f32) * (dp - Dp[pl.ds(i, 1)])).astype(bf16)
            dv[ksl, hs] = dot(e, do, NT).astype(bf16)
            dk[ksl, hs] = (dot(ds, qs[qsl, hs]) * (1.0 / LOG2E)).astype(bf16)
            dqT = (dot(kT[hs, ksl], ds) * scale).astype(bf16)
            dq[qsl, hs] = dqT.T

    def weight_grads(m):
        cols = pl.ds(m * 256, 256)
        acc = jnp.zeros((D, 256), f32)
        for t in range(2):
            sup = pl.multiple_of(t * HALF + f * QUART, QUART)
            acc += dot(a1s[pl.ds(sup, QUART)], dq[pl.ds(t * 512, QUART), cols], TN)
            acc += dot(a1q[pl.ds(t * QUART, QUART)], dq[pl.ds(t * 512 + QUART, QUART), cols], TN)
        put(m, 0, acc.astype(bf16))
        put(m, 1, dot(a1s[...], dk[:, cols], TN).astype(bf16))
        put(m, 2, dot(a1s[...], dv[:, cols], TN).astype(bf16))

    heads(0)
    heads(1)
    weight_grads(0)
    core_copy(2).start()
    heads(2)
    step(2, 0)
    step(0, 1)
    heads(3)
    weight_grads(1)
    core_copy(3).start()
    step(0, 2)

    sg[...] = sgF[...]
    eg[...] = jnp.zeros_like(eg)
    gain = small[1:2]
    emb_cols = pl.ds(2 * HALF, D)

    def back(da, nrm, rstd, extra, cols, out_cols):
        sg[1:2] += jnp.sum(da * nrm, axis=0, keepdims=True)
        sg[2:3] += jnp.sum(da, axis=0, keepdims=True)
        cc = da * gain
        m1 = jnp.mean(cc, axis=-1, keepdims=True)
        m2 = jnp.mean(cc * nrm, axis=-1, keepdims=True)
        wide = jnp.concatenate([rstd] * 4, axis=1)
        dh = wide * (cc - m1 - nrm * m2)
        if extra is not None:
            dh = dh + extra
        sg[0:1] += jnp.sum(dh, axis=0, keepdims=True)
        de = dh.astype(bf16)
        part = dot(XT[:, cols], de)
        back_in = dot(XT[:, emb_cols], de, NT).astype(bf16)
        for k in range(4):
            eg[k] += part[k * PADF:(k + 1) * PADF]
            GT[k % 2, k // 2, :, out_cols] = back_in[k * PADF:(k + 1) * PADF]

    def below(t):
        q0 = t * 512
        wq, wk, wv = W4[pl.ds(0, D)], W4[pl.ds(D, D)], W4[pl.ds(2 * D, D)]
        da = dot(dq[pl.ds(q0 + QUART, QUART)], wq, NT)
        p0 = pl.ds(t * QUART, QUART)
        back(
            da, n1q[p0].astype(f32), rq[p0], dy1[pl.ds(q0 + QUART, QUART)],
            pl.ds(2 * HALF + D + t * QUART, QUART), pl.ds(2 * HALF + t * QUART, QUART),
        )
        for b in range(4):
            rows = pl.ds(pl.multiple_of(t * HALF + ((f + b) % 4) * QUART, QUART), QUART)
            da = dot(dk[rows], wk, NT) + dot(dv[rows], wv, NT)
            extra = None
            if b == 0:
                da = da + dot(dq[pl.ds(q0, QUART)], wq, NT)
                extra = dy1[pl.ds(q0, QUART)]
            back(da, n1s[rows].astype(f32), rs[rows], extra, rows, rows)

    below(0)
    step(3, 0)
    step(1, 1)
    step(0, 3)
    below(1)

    small_rows = pl.ds(0, 16)
    PK[0, small_rows] = sg[...]
    for k in range(2):
        PK[0, pl.ds(16 + k * PADF, PADF)] = eg[2 * k + 1 - c]
    def pk_copy(i, rows):
        dev = core_id if i == 0 else x_id if i == 1 else row_id[i - 2]
        return remote(PK.at[i, pl.ds(0, rows)], RK.at[i, pl.ds(0, rows)], ps.at[i], pr.at[i], dev)

    def pk_step(i):
        pk_copy(i, 80 if i == 0 else 48).wait_recv()
        if i == 0:
            PK[1, small_rows] = PK[0, small_rows] + RK[0, small_rows]
            own = [eg[2 * k + c] + RK[0, pl.ds(16 + k * PADF, PADF)] for k in range(2)]
            keep = jnp.where(x == 0, own[0], own[1])
            PK[1, pl.ds(16, PADF)] = jnp.where(x == 0, own[1], own[0])
            PK[1, pl.ds(48, PADF)] = keep
            pk_copy(1, 48).start()
        else:
            old = PK[1, pl.ds(48, PADF)] if i == 1 else PK[i, pl.ds(16, PADF)]
            a = PK[i, small_rows] + RK[i, small_rows]
            b = old + RK[i, pl.ds(16, PADF)]
            if i < n + 1:
                PK[i + 1, small_rows] = a
                PK[i + 1, pl.ds(16, PADF)] = b
                pk_copy(i + 1, 48).start()
            else:
                SM[...] = a
                EM[...] = b

    pk_copy(0, 80).start()
    gt1 = remote(GT.at[1 - c], GC, gs.at[0], gr.at[0], core_id)
    gt1.start()
    sup = pl.ds(0, 2 * HALF)
    que = pl.ds(2 * HALF, 512)

    def que_of(k, first=2 * HALF):
        return pl.ds(pl.multiple_of(first + k * 512, 512), 512)

    gt2 = remote(XS, XR, gs.at[1], gr.at[1], x_id)
    step(0, 4)
    step(2, 1)
    pk_step(0)
    gt1.wait_recv()
    XS[:, sup] = (GT[c, 1 - x, :, sup].astype(f32) + GC[1 - x, :, sup].astype(f32)).astype(bf16)
    XS[:, que_of(c)] = GT[c, 1 - x, :, que]
    XS[:, que_of(1 - c)] = GC[1 - x, :, que]
    gt2.start()
    step(3, 1)
    step(1, 2)
    pk_step(1)
    for st in range(3, 2 + 2 * n):
        step(1, st)
        step(2, st - 1)
        step(3, st - 1)
        if st + 2 < 2 + 2 * n:
            step(0, st + 2)
        if st - 1 < 2 + n:
            pk_step(st - 1)
    step(2, 1 + 2 * n)
    step(3, 1 + 2 * n)
    gt2.wait_recv()
    GI[:, sup] = (
        GT[c, x, :, sup].astype(f32) + GC[x, :, sup].astype(f32) + XR[:, sup].astype(f32)
    ).astype(bf16)
    GI[:, que_of(f)] = GT[c, x, :, que]
    GI[:, que_of(f ^ 1)] = GC[x, :, que]
    for k in range(2):
        GI[:, que_of(2 * (1 - x) + k)] = XR[:, que_of(k)]

    for s in range(4):
        u = su[s]
        g = lax.rem(2 * lax.div(u, R) + 4, 6)
        p = lax.rem(u, R)
        keep = occ[s]
        for m in range(2):
            SEL[s, m] = (AGB[g + m, p].astype(f32) * keep).astype(bf16)
    fin = [
        remote(SEL, FIN.at[f], fs.at[0], fr.at[0], core_id),
        remote(SEL, FIN.at[f], fs.at[1], fr.at[1], x_id),
        remote(FIN.at[f ^ 2], FIN.at[f ^ 2], fs.at[2], fr.at[2], core_id),
    ]
    mine = pltpu.make_async_copy(SEL, FIN.at[f], osem)
    fin[1].start()
    fin[0].start()
    mine.start()
    fin[1].wait_recv()
    fin[2].start()
    mine.wait()
    fin[0].wait()
    fin[1].wait_send()
    fin[2].wait()
    for k in range(4):
        core_copy(k).wait_send()
        x_copy(k).wait_send()
        for j in range(n):
            rs_copy(k, j).wait_send()
            ag_copy(k, j).wait_send()
    for i in range(n + 2):
        pk_copy(i, 80 if i == 0 else 48).wait_send()
    gt1.wait_send()
    gt2.wait_send()


def backward_call(R, gF, su, occ, dy1, W4, ET, linv, OT, q, k, kT, v, a1s, a1q, n1s, n1q, rs, rq, XT, small, sg):
    BH = gF.shape[4]
    n = R.bit_length() - 1
    sd = jax.ShapeDtypeStruct
    V = pltpu.VMEM
    dma = pltpu.SemaphoreType.DMA
    blk = (R, BH, 128)
    return pl.pallas_call(
        functools.partial(backward_kernel, R),
        out_shape=(sd((4, 4, 2, BH, 128), bf16), sd((16, D), f32), sd((PADF, D), f32), sd((PADF, 4096), bf16)),
        in_specs=[anyspace(), smem(), smem(), vmem(), vmem(), anyspace()] + [vmem()] * 15,
        out_specs=(anyspace(), vmem(), vmem(), vmem()),
        scratch_shapes=[
            V((8, HALF, 512), bf16), V((1024, D), bf16), V((D, 1024), bf16), V((8, 512), f32),
            V((1024, D), bf16), V((2048, D), bf16), V((2048, D), bf16), V((16, D), f32), V((4, PADF, D), f32),
            V((2, 2, PADF, 2560), bf16),
            V((2, 2, R, 2, BH, 128), bf16), V((4, R, 2, BH, 128), bf16), V((6, R, 2, BH, 128), bf16),
            V((2, 6) + blk, bf16), V((6,) + blk, bf16), V((6,) + blk, bf16), V((6,) + blk, bf16), V((6,) + blk, bf16),
            V((4, 2, BH, 128), bf16), V((n + 2, 80, D), f32), V((n + 2, 80, D), f32),
            V((2, PADF, 2560), bf16), V((PADF, 3072), bf16), V((PADF, 3072), bf16),
            dma((8,)), dma, dma((4, 2 + 2 * n)), dma((4, 2 + 2 * n)), dma((3,)), dma((3,)),
            dma((n + 2,)), dma((n + 2,)), dma((2,)), dma((2,)),
        ],
        compiler_params=pltpu.CompilerParams(collective_id=1, has_side_effects=True, vmem_limit_bytes=VMEM_BYTES),
        name="backward",
    )(gF, su, occ, dy1, W4, ET, linv, OT, q, k, kT, v, a1s, a1q, n1s, n1q, rs, rq, XT, small, sg)


def adamw(weight, grad, first, second, rate):
    first_new = BETA_FIRST * first + (1.0 - BETA_FIRST) * grad
    second_new = BETA_SECOND * second + (1.0 - BETA_SECOND) * grad * grad
    first_hat = first_new / (1.0 - BETA_FIRST**STEP)
    second_hat = second_new / (1.0 - BETA_SECOND**STEP)
    weight_new = weight - rate * (first_hat / (jnp.sqrt(second_hat) + ADAM_EPS) + DECAY * weight)
    return (first_new, second_new, weight_new)


def update_kernel(
    occ, tmap, FIN, w, m, v, SM, sw, sm, sv, EM, ew, em, ev, GI, masks,
    g_o, m_o, v_o, w_o, wc_o, eg_o, em_o, ev_o, ew_o, ec_o, sg_o, sm_o, sv_o, sw_o, gi_o,
):
    s = pl.program_id(0)
    keep = occ[s]
    BH = FIN.shape[3]
    for f in range(4):
        rows = pl.ds((f // 2) * BH, BH)
        for k in range(2):
            cols = pl.ds(k * 256 + (f % 2) * 128, 128)
            g = FIN[f, 0, k].astype(f32)
            a, b, d = adamw(w[0, rows, cols], g, m[0, rows, cols], v[0, rows, cols], RATE_MATRIX)
            g_o[0, rows, cols] = g * keep
            m_o[0, rows, cols] = a * keep
            v_o[0, rows, cols] = b * keep
            d = d * keep
            w_o[0, rows, cols] = d
            wc_o[0, rows, cols] = d.astype(bf16)

    @pl.when(s == 0)
    def _():
        g = SM[0:10]
        a, b, d = adamw(sw[...], g, sm[...], sv[...], RATE_SMALL)
        sg_o[...] = g
        sm_o[...] = a
        sv_o[...] = b
        sw_o[...] = d
        nf = ew.shape[0]
        g = EM[pl.ds(0, nf)]
        a, b, d = adamw(ew[...], g, em[...], ev[...], RATE_EMBED)
        eg_o[...] = g
        em_o[...] = a
        ev_o[...] = b
        ew_o[...] = d
        ec_o[...] = d.astype(bf16)

    nf = gi_o.shape[3]
    T = masks.shape[0]
    row_iota = lax.broadcasted_iota(jnp.int32, (T, nf), 0)
    t = s // 2
    line = jnp.sum(jnp.where(row_iota == tmap[t], masks[...], 0), axis=0, keepdims=True)
    eye = jnp.where(
        lax.broadcasted_iota(jnp.int32, (PADF, nf), 0) == lax.broadcasted_iota(jnp.int32, (PADF, nf), 1),
        jnp.broadcast_to(line, (PADF, nf)), 0,
    ).astype(f32).astype(bf16)

    @pl.when(s % 2 == 0)
    def _():
        cols = pl.ds(pl.multiple_of(t * HALF, HALF), HALF)
        gi_o[0, 0] = dot(GI[:, cols], eye, TN).astype(bf16)

    @pl.when(s % 2 == 1)
    def _():
        for k in range(4):
            cols = pl.ds(pl.multiple_of(2 * HALF + k * 512 + t * QUART, QUART), QUART)
            gi_o[0, 0, pl.ds(k * QUART, QUART)] = dot(GI[:, cols], eye, TN).astype(bf16)


def update_call(occ, tmap, FIN, w, m, v, SM, sw, sm, sv, EM, ew, em, ev, GI, masks):
    S, BR, W = w.shape
    nf = ew.shape[0]
    sd = jax.ShapeDtypeStruct
    blk = pl.BlockSpec((1, BR, W), lambda s: (s, 0, 0))
    whole = lambda a: pl.BlockSpec(a.shape, lambda s: (0,) * len(a.shape))
    ins = [smem(), smem(), pl.BlockSpec((4, 1, 2, BR // 2, 128), lambda s: (0, s, 0, 0, 0)), blk, blk, blk]
    ins += [whole(a) for a in (SM, sw, sm, sv, EM, ew, em, ev, GI, masks)]
    big = sd((S, BR, W), f32)
    small = sd((10, D), f32)
    e = sd((nf, D), f32)
    outs = [big, big, big, big, sd((S, BR, W), bf16), e, e, e, e, sd((nf, D), bf16), small, small, small, small, sd((2, 2, HALF, nf), bf16)]
    specs = [blk] * 5 + [whole(a) for a in outs[5:14]] + [pl.BlockSpec((1, 1, HALF, nf), lambda s: (s // 2, s % 2, 0, 0))]
    return pl.pallas_call(
        update_kernel, out_shape=tuple(outs), grid=(S,), in_specs=ins, out_specs=tuple(specs),
        compiler_params=pltpu.CompilerParams(vmem_limit_bytes=VMEM_BYTES), name="update",
    )(occ, tmap, FIN, w, m, v, SM, sw, sm, sv, EM, ew, em, ev, GI, masks)


def body(
    features, feature_masks, table_map, owners, out_grad, weight_slots, moment1_slots, moment2_slots,
    emb_weight, emb_moment1, emb_moment2, small_weight, small_moment1, small_moment2,
):
    unit_count = owners.shape[0]
    capacity, block_rows, width = weight_slots.shape
    R = lax.axis_size("rows")
    bits = R.bit_length() - 1
    my_row = lax.axis_index("rows")
    units = jnp.arange(unit_count, dtype=jnp.int32)
    same_owner = owners[:, None] == owners[None, :]
    owner_rank = jnp.sum((same_owner & (units[None, :] < units[:, None])).astype(jnp.int32), axis=1)
    distance = owners ^ my_row
    place = jnp.zeros_like(distance)
    for bit in range(bits):
        place = place | (((distance >> bit) & 1) << (bits - 1 - bit))
    pos = place * capacity + owner_rank
    slot_iota = jnp.arange(capacity, dtype=jnp.int32)
    hit = (owners[None, :] == my_row) & (owner_rank[None, :] == slot_iota[:, None])
    slot_unit = jnp.sum(jnp.where(hit, units[None, :], 0), axis=1)
    occupied = jnp.sum(hit.astype(f32), axis=1)

    G, XT, h0o, a1s, a1q, n1s, n1q, rs, rq = gather_call(
        R, weight_slots, features, feature_masks, table_map, emb_weight, small_weight
    )
    G = G.reshape(R * capacity, block_rows, width)
    dY = out_grad.reshape(1024, width)
    out, gF, dy1, sg, ET, linv, OT, q, k, kT, v, W4 = forward_call(pos, G, h0o, a1s, a1q, dY, small_weight)
    FIN, SM, EM, GI = backward_call(
        R, gF, slot_unit, occupied, dy1, W4, ET, linv, OT, q, k, kT, v, a1s, a1q, n1s, n1q, rs, rq, XT, small_weight, sg
    )
    (
        g_slots, m_slots, v_slots, w_slots, w_copy, e_grad, e_m, e_v, e_w, e_copy, s_grad, s_m, s_v, s_w, grad_inputs,
    ) = update_call(
        occupied, table_map, FIN, weight_slots, moment1_slots, moment2_slots, SM, small_weight, small_moment1,
        small_moment2, EM, emb_weight, emb_moment1, emb_moment2, GI, feature_masks,
    )
    return (
        out.reshape(out_grad.shape), grad_inputs, g_slots, m_slots, v_slots, w_slots, w_copy,
        e_grad, e_m, e_v, e_w, e_copy, s_grad, s_m, s_v, s_w,
    )


def solution(mesh):
    rows3 = P("rows", None, None)
    feat2 = P("feat", None)
    in_specs = (
        P("rows", None, None, "feat"), P(None, "feat"), P("rows"), P(), P("rows", None, "feat", None),
        rows3, rows3, rows3, feat2, feat2, feat2, P(), P(), P(),
    )
    out_specs = (
        P("rows", None, "feat", None), P("rows", None, None, "feat"), rows3, rows3, rows3, rows3, rows3,
        feat2, feat2, feat2, feat2, feat2, P(), P(), P(), P(),
    )
    return jax.shard_map(body, mesh=mesh, in_specs=in_specs, out_specs=out_specs, check_vma=False)
```

time: 656 us -> 215 us (0.33)
  waiting for transfers between devices: 257 us -> 0 us
  Pallas kernels: 0 us -> 205 us
  matrix products: 122 us -> 0 us
  local copies, waits for them, and re-layouts: 101 us -> 4.38 us
  blocking collectives: 95.6 us -> 0 us
  other arithmetic: 50.2 us -> 4.01 us
  between operations: 16.1 us -> 0.68 us
  starting transfers between devices: 9.63 us -> 0 us
    pallas_call x0 -> x4, Pallas kernels: none -> 205 us  [the longest x1 92.2 us: backward_call(): pl.pallas_call(functools.partial(backward_kernel, R), out_shape=(sd((4, 4...]
    dot_general x38 -> x0, matrix products: 122 us -> none  [the longest x1 20.7 us: body(): jnp.dot(act2, w_up, preferred_element_type=jnp.float32)]
    all_gather x3 -> x0, waiting for transfers between devices: 117 us -> none  [the longest x1 101 us: body(): lax.all_gather(weight_slots.astype(jnp.bfloat16), 'rows', axis=0, tiled=T...]
    psum x1 -> x0, waiting for transfers between devices: 114 us -> none  [body(): lax.psum((grad_stack, small_terms), ('feat', 'rows'))]
    psum x2 -> x0, blocking collectives: 80.3 us -> none  [the longest x1 42.6 us: body(): lax.psum((grad_stack, small_terms), ('feat', 'rows'))]
    convert_element_type x9 -> x0, other arithmetic: 35.3 us -> none  [the longest x1 20.8 us: body(): gelu_low = gelu_out.astype(jnp.bfloat16)]
    reduce_scatter x2 -> x0, waiting for transfers between devices: 25.1 us -> none  [the longest x1 25.1 us: body(): lax.psum_scatter(value_terms.astype(jnp.bfloat16), 'feat', scatter_dimens...]
    slice x9 -> x0, local copies, waits for them, and re-layouts: 18.2 us -> none  [the longest x2 6.31 us: body(): w_up = matrices[4:8].transpose(1, 0, 2).reshape(width, 4 * width)]
  transfers between devices with their start and end apart: 9 -> 0, of which waited for: 4 -> 0; matrix products, arithmetic and copies ran while one was open for 18% -> 0% of each run, Pallas kernels for 0% -> 0%
where the time goes in v2:
time: 215 us; the launch traced here: 214 us
  Pallas kernels  205 us (95%)
  local copies, waits for them, and re-layouts  4.38 us (2%)
  other arithmetic  4.01 us (2%)
    pallas_call x1, Pallas kernels, backward_call(): pl.pallas_call(functools.partial(backward_kernel, R), out_shape=(sd((4, 4...  92.2 us
    pallas_call x1, Pallas kernels, gather_call(): pl.pallas_call(functools.partial(gather_kernel, R), out_shape=(sd((R, S,...  59.7 us
    pallas_call x1, Pallas kernels, forward_call(): pl.pallas_call(functools.partial(forward_kernel, BR), out_shape=(sd((1024...  43.8 us
    pallas_call x1, Pallas kernels, update_call(): pl.pallas_call(update_kernel, out_shape=tuple(outs), grid=(S,), in_specs=...  9.23 us
    unnamed x2, local copies, waits for them, and re-layouts  4.38 us

profile of v2, /device:TPU:0, one launch (start us, length us, event | category | flops | bytes accessed | tf_op | source)
XLA Modules:
  0.0 214.0 jit_solution(7370026863910935083)
XLA Ops:
  0.6 0.9 convert_reduce_fusion
  1.6 0.7 broadcast_compare_fusion
  2.2 1.2 multiply_add_fusion.pos
  3.4 0.6 convert_reduce_fusion.1.occ
  4.0 0.6 select_reduce_fusion.su
  4.7 2.2 %copy.32.feat_ref = bf16[2,2,1024,25]{3,2,1,0:T(8,128)(2,1)} copy(bf16[2,2,1024,25]{2,1,3,0:T(2,128)(2,1)} %param.14) | data formatting | bytes 409600 | tf_op args[0]
  6.9 59.7 %gather_weights.1 = (bf16[8,4,256,512]{3,2,1,0:T(8,128)(2,1)}, bf16[128,3072]{1,0:T(8,128)(2,1)}, f32[1024,512]{1,0:T(8,128)}, bf16[2048,512]{1,0:T(8,128)(2,1)}...) custom-call(f32[4,256,512]{2,1,0:T(8,128)} %w.1, ...), custom_call_target="tpu_custom_call" | custom-call | tf_op jit(solution)/shard_map/gather_weights/pallas_call | solution.py:246
  66.5 43.8 %forward.1 = (bf16[1024,512]{1,0:T(8,128)(2,1)}, bf16[4,2,8,2,128,128]{5,4,3,2,1,0:T(8,128)(2,1)}, f32[1024,512]{1,0:T(8,128)}, f32[16,512]{1,0:T(8,128)}, bf16[...) custom-call(s32[24]{0:T(128)} %multiply_add_fusion.pos, ...), custom_call_target="tpu_custom_call" | custom-call | tf_op jit(solution)/shard_map/forward/pallas_call | solution.py:416
  110.3 92.2 %backward.1 = (bf16[4,4,2,128,128]{4,3,2,1,0:T(8,128)(2,1)}, f32[16,512]{1,0:T(8,128)}, f32[32,512]{1,0:T(8,128)}, bf16[32,4096]{1,0:T(8,128)(2,1)}) custom-call(bf16[4,2,8,2,128,128]{5,4,3,2,1,0:T(8,128)(2,1)} %get-tuple-element.61.gF, s32[4]{0:T(128)} %select_reduce_fusion.su, f32[4]{0:T(128)} %convert_reduce_fusion.1.occ, ...), custom_call_target="tpu_custom_call" | custom-call | tf_op jit(solution)/shard_map/backward/pallas_call | solution.py:761
  202.6 9.2 %update.1 = (f32[4,256,512]{2,1,0:T(8,128)}, f32[4,256,512]{2,1,0:T(8,128)}, f32[4,256,512]{2,1,0:T(8,128)}, f32[4,256,512]{2,1,0:T(8,128)}, bf16[4,256,512]{2,1...) custom-call(f32[4]{0:T(128)} %convert_reduce_fusion.1.occ, ...), custom_call_target="tpu_custom_call" | custom-call | tf_op jit(solution)/shard_map/update/pallas_call | solution.py:863
  211.8 2.2 %copy.33 = bf16[2,2,1024,25]{2,1,3,0:T(2,128)(2,1)} copy(bf16[2,2,1024,25]{3,2,1,0:T(8,128)(2,1)} %get-tuple-element.113) | data formatting | bytes 409600

commit v3 on v2

v3 whole, which is shorter than its diff:
```python
import functools
import math

import jax
import jax.numpy as jnp
from jax import lax
from jax.experimental import pallas as pl
from jax.experimental.pallas import tpu as pltpu
from jax.sharding import PartitionSpec as P

MESH = pl.DeviceIdType.MESH
bf16, f32 = jnp.bfloat16, jnp.float32
NN = (((1,), (0,)), ((), ()))
NT = (((1,), (1,)), ((), ()))
TN = (((0,), (0,)), ((), ()))
LOG2E = math.log2(math.e)
HEADS = 4
HEAD_DIM = 128
STEP = 10
LN_EPS = 1e-05
BETA_FIRST = 0.9
BETA_SECOND = 0.999
ADAM_EPS = 1e-08
DECAY = 0.01
RATE_MATRIX = 0.1
RATE_EMBED = 0.3
RATE_SMALL = 0.6
D = 512
HALF = 1024
QUART = 256
PADF = 32
VMEM_BYTES = 60 * 2**20


def dot(a, b, dims=NN):
    return lax.dot_general(a, b, dims, preferred_element_type=f32)


def vmem():
    return pl.BlockSpec(memory_space=pltpu.VMEM)


def anyspace():
    return pl.BlockSpec(memory_space=pl.ANY)


def smem():
    return pl.BlockSpec(memory_space=pltpu.SMEM)


def remote(src, dst, send, recv, dev):
    return pltpu.make_async_remote_copy(
        src_ref=src, dst_ref=dst, send_sem=send, recv_sem=recv, device_id=dev, device_id_type=MESH
    )


def greet(peers):
    bar = pltpu.get_barrier_semaphore()
    for d in peers:
        pl.semaphore_signal(bar, inc=1, device_id=d, device_id_type=MESH)
    return bar


def mask_column(masks, table):
    which = lax.broadcasted_iota(jnp.int32, masks.shape, 1) == table
    return jnp.sum(jnp.where(which, masks[...], 0), axis=1, keepdims=True).astype(f32)


GROUPS = ((1, 3, True), (0, 1, False))


def gather_kernel(
    R, slots_ref, feat_ref, mask_ref, tmap_ref, emb_ref, small_ref,
    G_ref, XT_ref, h0_ref, a1s_ref, a1q_ref, n1s_ref, n1q_ref, rs_ref, rq_ref,
    own, XTo, XTa, tmpq, lsem, fs, fr, hs, hr, xs, xr, cs, cr, c2s, c2r,
):
    f = lax.axis_index("feat")
    r = lax.axis_index("rows")
    x = f // 2
    c = f % 2
    n = R.bit_length() - 1
    S, BR, W = own.shape
    BH, CH = BR // 2, W // 2
    core_id = (f ^ 1, r)
    x_id = (f ^ 2, r)
    row_id = [(f, r ^ (1 << (n - 1 - j))) for j in range(n)]
    peers = [core_id, x_id] + row_id
    bar = greet(peers)
    own[...] = slots_ref[...].astype(bf16)
    pl.semaphore_wait(bar, len(peers))
    local = pltpu.make_async_copy(own, G_ref.at[0], lsem)
    local.start()
    subs = [(j, g) for j in range(n) for g in range(-1, j)]
    index = {jg: i for i, jg in enumerate(subs)}

    def span(g):
        return (0, 1) if g < 0 else (1 << g, 1 << g)

    def region(s, half_col):
        rows = pl.ds(pl.multiple_of(c * BH, BH), BH)
        cols = pl.ds(pl.multiple_of(half_col * CH, CH), CH) if GROUPS[s][2] else pl.ds(0, W)
        return pl.ds(GROUPS[s][0], GROUPS[s][1]), rows, cols

    def hyper(s, j, g):
        where = region(s, x)
        start, size = span(g)
        k = index[(j, g)]
        if g < 0:
            src, dst = own.at[where], G_ref.at[(1 << j, *where)]
        else:
            src = G_ref.at[(pl.ds(start, size), *where)]
            dst = G_ref.at[(pl.ds((1 << j) + start, size), *where)]
        return remote(src, dst, hs.at[s, k], hr.at[s, k], row_id[j])

    def forward(s, j, g, half_col, sems, semr, dev):
        start, size = span(g)
        k = index[(j, g)]
        ref = G_ref.at[(pl.ds((1 << j) + start, size), *region(s, half_col))]
        return remote(ref, ref, sems.at[s, k], semr.at[s, k], dev)

    order = range(len(GROUPS))
    for s in order:
        for j in range(n):
            hyper(s, j, -1).start()

    nf = feat_ref.shape[1]
    XTo[...] = jnp.zeros_like(XTo)
    for t in range(2):
        keep = mask_column(mask_ref, tmap_ref[t])
        XTo[pl.ds(0, nf), pl.ds(t * HALF, HALF)] = (feat_ref[t, :, 0, :].astype(f32) * keep).astype(bf16)
        query = (feat_ref[t, :, 1, :].astype(f32) * keep).astype(bf16)
        for k in range(4):
            XTo[pl.ds(0, nf), pl.ds(2 * HALF + D + k * 512 + t * QUART, QUART)] = query[:, k * QUART:(k + 1) * QUART]
    XTo[pl.ds(0, nf), pl.ds(2 * HALF, D)] = emb_ref[...].astype(bf16)
    wide = 2 * HALF + D
    shared = pl.ds(0, wide)

    def rows_of(dev):
        return pl.ds(pl.multiple_of(dev * PADF, PADF), PADF)

    def chunk_of(dev):
        return pl.ds(pl.multiple_of(wide + dev * 512, 512), 512)

    tail = pl.ds(wide, 512)
    feats = [
        remote(XTo.at[:, shared], XTa.at[rows_of(f), shared], fs.at[0], fr.at[0], core_id),
        remote(XTo.at[:, chunk_of(f ^ 1)], XTa.at[rows_of(f), tail], fs.at[1], fr.at[1], core_id),
        remote(XTo.at[:, shared], XTa.at[rows_of(f), shared], fs.at[2], fr.at[2], x_id),
        remote(XTo.at[:, chunk_of(f ^ 2)], XTa.at[rows_of(f), tail], fs.at[3], fr.at[3], x_id),
        remote(XTo.at[:, chunk_of(f ^ 3)], tmpq, fs.at[4], fr.at[4], x_id),
        remote(XTa.at[rows_of(f ^ 2), shared], XTa.at[rows_of(f ^ 2), shared], fs.at[5], fr.at[5], core_id),
        remote(tmpq, XTa.at[rows_of(f ^ 2), tail], fs.at[6], fr.at[6], core_id),
    ]
    for copy in feats[:5]:
        copy.start()
    XTa[rows_of(f), shared] = XTo[:, shared]
    XTa[rows_of(f), tail] = XTo[:, chunk_of(f)]

    def x_arrive(j):
        for s in order:
            if GROUPS[s][2]:
                for g in range(-1, j):
                    forward(s, j, g, x, xs, xr, x_id).wait_recv()
                    forward(s, j, g, 1 - x, c2s, c2r, core_id).start()

    def hyper_arrive(j):
        for s in order:
            for g in range(-1, j):
                hyper(s, j, g).wait_recv()
                if GROUPS[s][2]:
                    forward(s, j, g, x, xs, xr, x_id).start()
                forward(s, j, g, x, cs, cr, core_id).start()
            for j2 in range(j + 1, n):
                hyper(s, j2, j).start()

    hyper_arrive(0)
    feats[2].wait_recv()
    feats[4].wait_recv()
    feats[5].start()
    feats[6].start()
    for j in range(1, n - 1):
        hyper_arrive(j)
        x_arrive(j - 1)
    for k in (0, 1, 3, 5, 6):
        feats[k].wait_recv()

    shift0 = small_ref[0:1]
    gain = small_ref[1:2]
    shift = small_ref[2:3]
    E = XTa[:, pl.ds(2 * HALF, D)]

    def norm(cols):
        h = dot(XTa[:, cols], E, TN) + shift0
        mean = jnp.mean(h, axis=-1, keepdims=True)
        cen = h - mean
        rstd = lax.rsqrt(jnp.mean(cen * cen, axis=-1, keepdims=True) + LN_EPS)
        nrm = cen * rstd
        return h, nrm, rstd, (nrm * gain + shift).astype(bf16)

    @pl.loop(0, 8)
    def _(i):
        rows = pl.ds(pl.multiple_of(i * QUART, QUART), QUART)
        h, nrm, rstd, act = norm(rows)
        n1s_ref[rows] = nrm.astype(bf16)
        a1s_ref[rows] = act
        rs_ref[rows] = jnp.broadcast_to(rstd, (QUART, 128))

        @pl.when(i % 4 == f)
        def _():
            h0_ref[pl.ds(pl.multiple_of((i // 4) * 512, 512), QUART)] = h

    @pl.loop(0, 2)
    def _(t):
        rows = pl.ds(pl.multiple_of(t * QUART, QUART), QUART)
        h, nrm, rstd, act = norm(pl.ds(pl.multiple_of(wide + t * QUART, QUART), QUART))
        n1q_ref[rows] = nrm.astype(bf16)
        a1q_ref[rows] = act
        rq_ref[rows] = jnp.broadcast_to(rstd, (QUART, 128))
        h0_ref[pl.ds(pl.multiple_of(t * 512 + QUART, QUART), QUART)] = h

    XT_ref[...] = XTa[...]
    hyper_arrive(n - 1)
    if n > 1:
        x_arrive(n - 2)
    x_arrive(n - 1)
    local.wait()
    for copy in feats:
        copy.wait_send()
    for s in order:
        for j, g in subs:
            hyper(s, j, g).wait_send()
            forward(s, j, g, x, cs, cr, core_id).wait()
            if GROUPS[s][2]:
                forward(s, j, g, x, xs, xr, x_id).wait_send()
                forward(s, j, g, 1 - x, c2s, c2r, core_id).wait()


def gather_call(R, slots, features, masks, tmap, emb, small):
    S, BR, W = slots.shape
    n = R.bit_length() - 1
    M = n * (n + 1) // 2
    sem = pltpu.SemaphoreType.DMA((len(GROUPS), M))
    sd = jax.ShapeDtypeStruct
    cols = 2 * HALF + D + 512
    return pl.pallas_call(
        functools.partial(gather_kernel, R),
        out_shape=(
            sd((R, S, BR, W), bf16), sd((4 * PADF, cols), bf16), sd((1024, D), f32),
            sd((2048, D), bf16), sd((512, D), bf16), sd((2048, D), bf16), sd((512, D), bf16),
            sd((2048, 128), f32), sd((512, 128), f32),
        ),
        in_specs=[vmem(), vmem(), vmem(), smem(), vmem(), vmem()],
        out_specs=(anyspace(),) + (vmem(),) * 8,
        scratch_shapes=[
            pltpu.VMEM((S, BR, W), bf16), pltpu.VMEM((PADF, 2 * HALF + D + 2048), bf16),
            pltpu.VMEM((4 * PADF, cols), bf16), pltpu.VMEM((PADF, 512), bf16),
            pltpu.SemaphoreType.DMA, pltpu.SemaphoreType.DMA((7,)), pltpu.SemaphoreType.DMA((7,)),
        ] + [sem] * 8,
        compiler_params=pltpu.CompilerParams(collective_id=0, has_side_effects=True, vmem_limit_bytes=VMEM_BYTES),
        name="gather_weights",
    )(slots, features, masks, tmap, emb, small)


def gelu_pair(u):
    t = 1.0 / (1.0 + (0.3275911 * math.sqrt(0.5)) * jnp.abs(u))
    ex = jnp.exp2((-0.5 * LOG2E) * (u * u))
    poly = t * (0.127414796 + t * (-0.142248368 + t * (0.7107068705 + t * (-0.7265760135 + t * 0.5307027145))))
    e = poly * ex
    phi = jnp.where(u >= 0, 1.0 - e, e)
    return u * phi, phi + u * ex * (1.0 / math.sqrt(2 * math.pi))


def forward_kernel(
    BR, pos, G, a1s, a1q,
    Wo, linv, qo, kTo, vo, ET, OT, Oo,
    W, q_s, k_s, kT_s, v_s, vT_s, ET_s, OT_s, O_s, wsem, osem,
):
    U = pos.shape[0]
    R = U // 3
    per = D // BR
    f = lax.axis_index("feat")

    def wcopy(u):
        return pltpu.make_async_copy(G.at[pos[u]], W.at[pl.ds(u * BR, BR)], wsem.at[u])

    for u in range(U):
        wcopy(u).start()

    def wwait(i):
        for u in range(i * per, (i + 1) * per):
            wcopy(u).wait()

    def mat(i):
        return W[pl.ds(i * D, D)]

    scale = (HEAD_DIM**-0.5) * LOG2E
    outs = []

    def ship(src, dst):
        copy = pltpu.make_async_copy(src, dst, osem.at[len(outs)])
        copy.start()
        outs.append(copy)

    wwait(0)
    for t in range(2):
        sup = pl.multiple_of(t * HALF + f * QUART, QUART)
        q_s[pl.ds(t * 512, QUART)] = (dot(a1s[pl.ds(sup, QUART)], mat(0)) * scale).astype(bf16)
        q_s[pl.ds(t * 512 + QUART, QUART)] = (dot(a1q[pl.ds(t * QUART, QUART)], mat(0)) * scale).astype(bf16)
    wwait(1)
    wwait(2)

    @pl.loop(0, 4)
    def _(i):
        rows = pl.ds(pl.multiple_of(i * 512, 512), 512)
        a = a1s[rows]
        k = dot(a, mat(1)).astype(bf16)
        k_s[rows] = k
        kT_s[:, rows] = k.T
        v = dot(a, mat(2)).astype(bf16)
        v_s[rows] = v
        vT_s[:, rows] = v.T

    ship(q_s, qo)
    ship(kT_s, kTo)
    ship(v_s, vo)
    for i in range(3, 12):
        wwait(i)
    ship(W, Wo)

    @pl.loop(0, 8)
    def _(i):
        t = i // HEADS
        h = i % HEADS
        ks = pl.ds(pl.multiple_of(t * HALF, HALF), HALF)
        qs = pl.ds(pl.multiple_of(t * 512, 512), 512)
        hs = pl.ds(pl.multiple_of(h * HEAD_DIM, HEAD_DIM), HEAD_DIM)
        st = dot(k_s[ks, hs], q_s[qs, hs], NT)
        top = jnp.max(st, axis=0, keepdims=True)
        e = jnp.exp2(st - top)
        inv = 1.0 / jnp.sum(e, axis=0, keepdims=True)
        eb = e.astype(bf16)
        ET_s[i] = eb
        pltpu.make_async_copy(ET_s.at[i], ET.at[i], osem.at[6 + i]).start()
        linv[pl.ds(i, 1)] = inv
        ot = (dot(vT_s[hs, ks], eb) * inv).astype(bf16)
        OT_s[hs, qs] = ot
        O_s[qs, hs] = ot.T

    ship(O_s, Oo)
    ship(OT_s, OT)
    for copy in outs:
        copy.wait()
    for i in range(8):
        pltpu.make_async_copy(ET_s.at[i], ET.at[i], osem.at[6 + i]).wait()


def forward_call(pos, G, a1s, a1q):
    BR = G.shape[1]
    U = pos.shape[0]
    sd = jax.ShapeDtypeStruct
    V = pltpu.VMEM
    return pl.pallas_call(
        functools.partial(forward_kernel, BR),
        out_shape=(
            sd((12 * D, D), bf16), sd((8, 512), f32), sd((1024, D), bf16), sd((D, 2048), bf16), sd((2048, D), bf16),
            sd((8, HALF, 512), bf16), sd((D, 1024), bf16), sd((1024, D), bf16),
        ),
        in_specs=[smem(), anyspace(), vmem(), vmem()],
        out_specs=(anyspace(), vmem()) + (anyspace(),) * 6,
        scratch_shapes=[
            V((12 * D, D), bf16), V((1024, D), bf16), V((2048, D), bf16), V((D, 2048), bf16), V((2048, D), bf16),
            V((D, 2048), bf16), V((8, HALF, 512), bf16), V((D, 1024), bf16), V((1024, D), bf16),
            pltpu.SemaphoreType.DMA((U,)), pltpu.SemaphoreType.DMA((14,)),
        ],
        compiler_params=pltpu.CompilerParams(vmem_limit_bytes=VMEM_BYTES),
        name="forward",
    )(pos, G, a1s, a1q)


CHUNKS = ((2, 2), (0, 2), (4, 1), (5, 1))


def main_kernel(
    R, su, occ, linv, small, Wh, Oh, h0h, dYh, ETh, OTh, qh, kTh, vh, a1sh, a1qh, n1sh, n1qh, rsh, rqh, XTh,
    out, FIN, SM, EM, GI,
    W, O_s, y_s, dY, ETb, OT, qs, kT, vs, a1s, a1q, n1s, n1q, rs, rq, XT,
    a2_s, G_s, dU_s, Dp, sg, eg, GT, S, RC, RX, RH, AGB, AGL, SEL, PK, RK, GC, XS, XR,
    lsem, esem, osem, ss, sr, fs, fr, ps, pr, gs, gr,
):
    f = lax.axis_index("feat")
    r = lax.axis_index("rows")
    x = f // 2
    c = f % 2
    n = R.bit_length() - 1
    BH = S.shape[4]
    per = D // (2 * BH)
    core_id = (f ^ 1, r)
    x_id = (f ^ 2, r)
    row_id = [(f, r ^ (1 << j)) for j in range(n)]
    peers = [core_id, x_id] + row_id
    bar = greet(peers)

    loads = {}

    def load(name, src, dst):
        loads[name] = pltpu.make_async_copy(src, dst, lsem.at[len(loads)])
        loads[name].start()

    def rows_w(i):
        return pl.ds(i * D, D)

    load("O", Oh, O_s)
    load("h0", h0h, y_s)
    for i in (3, 4, 8, 5, 9, 6, 10, 7, 11):
        load(i, Wh.at[rows_w(i)], W.at[rows_w(i)])
    load("dY", dYh, dY)
    load("OT", OTh, OT)
    load("v", vh, vs)
    load("q", qh, qs)
    load("kT", kTh, kT)

    def ecopy(h, t):
        k = (h % 2) * 2 + t
        return pltpu.make_async_copy(ETh.at[t * HEADS + h], ETb.at[k], esem.at[k])

    for h in range(2):
        for t in range(2):
            ecopy(h, t).start()
    load("a1s", a1sh, a1s)
    load("a1q", a1qh, a1q)
    load("n1s", n1sh, n1s)
    load("n1q", n1qh, n1q)
    load("rs", rsh, rs)
    load("rq", rqh, rq)
    load("XT", XTh, XT)
    for i in range(3):
        load(i, Wh.at[rows_w(i)], W.at[rows_w(i)])
    pl.semaphore_wait(bar, len(peers))

    bits = [(r >> j) & 1 for j in range(n)]
    base = [0]
    for j in range(n):
        base.append(base[j] + bits[j] * (R >> (j + 1)))

    def groups(k):
        return pl.ds(CHUNKS[k][0], CHUNKS[k][1])

    def core_copy(k):
        return remote(S.at[1 - c, :, groups(k)], RC.at[:, groups(k)], ss.at[k, 0], sr.at[k, 0], core_id)

    def x_copy(k):
        return remote(S.at[c, 1 - x, groups(k)], RX.at[groups(k)], ss.at[k, 1], sr.at[k, 1], x_id)

    def rs_copy(k, j):
        half = R >> (j + 1)
        away = base[j] + (1 - bits[j]) * half
        off = R - (R >> j)
        return remote(
            S.at[c, x, groups(k), pl.ds(away, half)], RH.at[groups(k), pl.ds(off, half)],
            ss.at[k, 2 + j], sr.at[k, 2 + j], row_id[j],
        )

    def ag_copy(k, j):
        span = pl.ds(base[j + 1], R >> (j + 1))
        ref = AGB.at[groups(k), span] if k < 3 else AGL.at[span]
        return remote(ref, ref, ss.at[k, 2 + n + j], sr.at[k, 2 + n + j], row_id[j])

    def add(a, b):
        return (a.astype(f32) + b.astype(f32)).astype(bf16)

    def step(k, stage):
        g0, ng = CHUNKS[k]
        gl = range(g0, g0 + ng)
        if stage == 0:
            core_copy(k).wait_recv()
            for g in gl:
                S[c, 1 - x, g] = add(S[c, 1 - x, g], RC[1 - x, g])
            x_copy(k).start()
            for g in gl:
                S[c, x, g] = add(S[c, x, g], RC[x, g])
        elif stage == 1:
            x_copy(k).wait_recv()
            for g in gl:
                S[c, x, g] = add(S[c, x, g], RX[g])
            rs_copy(k, 0).start()
        elif stage < 2 + n:
            j = stage - 2
            half = R >> (j + 1)
            off = R - (R >> j)
            rs_copy(k, j).wait_recv()
            keep = pl.ds(base[j + 1], half)
            for g in gl:
                total = add(S[c, x, g, keep], RH[g, pl.ds(off, half)])
                if j < n - 1:
                    S[c, x, g, keep] = total
                elif k < 3:
                    AGB[g, keep] = total
                else:
                    AGL[keep] = total
            if j < n - 1:
                rs_copy(k, j + 1).start()
            else:
                ag_copy(k, n - 1).start()
        else:
            j = 2 * n + 1 - stage
            ag_copy(k, j).wait_recv()
            if j > 0:
                ag_copy(k, j - 1).start()

    last = 2 + 2 * n
    done = [0] * len(CHUNKS)

    def tick(k):
        if done[k] < last:
            step(k, done[k])
            done[k] += 1

    def put(g0, i, val):
        for k in range(val.shape[1] // 128):
            piece = val[:, k * 128:(k + 1) * 128].reshape(per, 2, BH, 128)
            for h in range(2):
                S[k % 2, h, g0 + k // 2, pl.ds(i * per, per)] = piece[:, h]

    gain2 = small[3:4]
    shift2 = small[4:5]
    RB = 256

    def norm2(y1):
        cen = y1 - jnp.mean(y1, axis=-1, keepdims=True)
        rstd = lax.rsqrt(jnp.mean(cen * cen, axis=-1, keepdims=True) + LN_EPS)
        return cen * rstd, rstd

    loads["O"].wait()
    loads["h0"].wait()
    loads[3].wait()

    @pl.loop(0, 1024 // RB)
    def _(i):
        rows = pl.ds(pl.multiple_of(i * RB, RB), RB)
        y1 = y_s[rows] + dot(O_s[rows], W[rows_w(3)])
        y_s[rows] = y1
        n2, _ = norm2(y1)
        a2 = (n2 * gain2 + shift2).astype(bf16)
        a2_s[rows] = a2
        acc = y1 + small[5:6]
        for j in range(4):
            @pl.when(i == 0)
            def _():
                loads[4 + j].wait()
                loads[8 + j].wait()
            gl, gp = gelu_pair(dot(a2, W[rows_w(4 + j)]) + small[6 + j:7 + j])
            gb = gl.astype(bf16)
            G_s[j, rows] = gb
            dU_s[j, rows] = gp.astype(bf16)
            acc = acc + dot(gb, W[rows_w(8 + j)])
        O_s[rows] = acc.astype(bf16)

    ship_out = pltpu.make_async_copy(O_s, out, osem.at[0])
    ship_out.start()
    loads["dY"].wait()
    for j in range(4):
        put(2, j, dot(G_s[j], dY[...], TN).astype(bf16))
    core_copy(0).start()

    sg[...] = jnp.zeros_like(sg)

    def backward_rows(first, count):
        @pl.loop(first, first + count)
        def _(i):
            rows = pl.ds(pl.multiple_of(i * RB, RB), RB)
            dy = dY[rows]
            da2 = jnp.zeros((RB, D), f32)
            for j in range(4):
                du = (dot(dy, W[rows_w(8 + j)], NT) * dU_s[j, rows].astype(f32)).astype(bf16)
                dU_s[j, rows] = du
                sg[6 + j:7 + j] += jnp.sum(du.astype(f32), axis=0, keepdims=True)
                da2 = da2 + dot(du, W[rows_w(4 + j)], NT)
            n2, rstd = norm2(y_s[rows])
            dyf = dy.astype(f32)
            sg[3:4] += jnp.sum(da2 * n2, axis=0, keepdims=True)
            sg[4:5] += jnp.sum(da2, axis=0, keepdims=True)
            sg[5:6] += jnp.sum(dyf, axis=0, keepdims=True)
            cc = da2 * gain2
            m1 = jnp.mean(cc, axis=-1, keepdims=True)
            m2 = jnp.mean(cc * n2, axis=-1, keepdims=True)
            y_s[rows] = dyf + rstd * (cc - m1 - n2 * m2)

    backward_rows(0, 2)
    tick(0)
    backward_rows(2, 2)
    for j in range(4):
        put(0, j, dot(a2_s[...], dU_s[j], TN).astype(bf16))
    core_copy(1).start()

    scale = HEAD_DIM**-0.5
    for i in range(2):
        dU_s[1, pl.ds(i * 512, 512)] = y_s[pl.ds(i * 512, 512)].astype(bf16)
    for name in ("OT", "v", "q", "kT", "a1s", "a1q"):
        loads[name].wait()
    put(4, 3, dot(OT[...], dU_s[1]).astype(bf16))
    for t in range(2):
        cols = pl.ds(t * 512, 512)
        for h in range(HEADS):
            rows = pl.ds(h * HEAD_DIM, HEAD_DIM)
            d = dot(W[pl.ds(3 * D + h * HEAD_DIM, HEAD_DIM)], dU_s[1, cols], NT) * linv[pl.ds(t * HEADS + h, 1)]
            Dp[pl.ds(t * HEADS + h, 1)] = jnp.sum(d * OT[rows, cols].astype(f32), axis=0, keepdims=True)
            dU_s[2, pl.ds(t * 512 + h * HEAD_DIM, HEAD_DIM)] = d.astype(bf16)
    tick(1)

    def heads(h):
        hs = pl.ds(h * HEAD_DIM, HEAD_DIM)
        for t in range(2):
            ecopy(h, t).wait()

        @pl.loop(0, 2)
        def _(t):
            i = t * HEADS + h
            ksl = pl.ds(pl.multiple_of(t * HALF, HALF), HALF)
            qsl = pl.ds(pl.multiple_of(t * 512, 512), 512)
            do = dU_s[2, pl.ds(pl.multiple_of(t * 512 + h * HEAD_DIM, HEAD_DIM), HEAD_DIM)]
            dp = dot(vs[ksl, hs], do)
            e = ETb[(h % 2) * 2 + t]
            ds = (e.astype(f32) * (dp - Dp[pl.ds(i, 1)])).astype(bf16)
            G_s[2 + t, :, hs] = dot(e, do, NT).astype(bf16)
            G_s[t, :, hs] = (dot(ds, qs[qsl, hs]) * (1.0 / LOG2E)).astype(bf16)
            dqT = (dot(kT[hs, ksl], ds) * scale).astype(bf16)
            dU_s[0, qsl, hs] = dqT.T

        if h + 2 < HEADS:
            for t in range(2):
                ecopy(h + 2, t).start()

    def weight_grads(m):
        cols = pl.ds(m * 256, 256)
        acc = jnp.zeros((D, 256), f32)
        for t in range(2):
            sup = pl.multiple_of(t * HALF + f * QUART, QUART)
            acc += dot(a1s[pl.ds(sup, QUART)], dU_s[0, pl.ds(t * 512, QUART), cols], TN)
            acc += dot(a1q[pl.ds(t * QUART, QUART)], dU_s[0, pl.ds(t * 512 + QUART, QUART), cols], TN)
        put(4 + m, 0, acc.astype(bf16))
        for k in range(2):
            total = dot(a1s[pl.ds(0, HALF)], G_s[2 * k, :, cols], TN) + dot(a1s[pl.ds(HALF, HALF)], G_s[2 * k + 1, :, cols], TN)
            put(4 + m, 1 + k, total.astype(bf16))

    heads(0)
    tick(0)
    heads(1)
    weight_grads(0)
    core_copy(2).start()
    tick(0)
    heads(2)
    tick(2)
    tick(0)
    tick(1)
    heads(3)
    weight_grads(1)
    core_copy(3).start()
    tick(0)
    tick(1)

    eg[...] = jnp.zeros_like(eg)
    gain1 = small[1:2]
    emb_cols = pl.ds(2 * HALF, D)
    for name in ("n1s", "n1q", "rs", "rq", "XT", 0, 1, 2):
        loads[name].wait()

    def back(da, nrm, rstd, extra, cols, out_cols):
        sg[1:2] += jnp.sum(da * nrm, axis=0, keepdims=True)
        sg[2:3] += jnp.sum(da, axis=0, keepdims=True)
        cc = da * gain1
        m1 = jnp.mean(cc, axis=-1, keepdims=True)
        m2 = jnp.mean(cc * nrm, axis=-1, keepdims=True)
        wide = jnp.concatenate([rstd] * 4, axis=1)
        dh = wide * (cc - m1 - nrm * m2)
        if extra is not None:
            dh = dh + extra
        sg[0:1] += jnp.sum(dh, axis=0, keepdims=True)
        de = dh.astype(bf16)
        part = dot(XT[:, cols], de)
        back_in = dot(XT[:, emb_cols], de, NT).astype(bf16)
        for k in range(4):
            eg[k] += part[k * PADF:(k + 1) * PADF]
            GT[k % 2, k // 2, :, out_cols] = back_in[k * PADF:(k + 1) * PADF]

    def below(t):
        q0 = t * 512
        wq, wk, wv = W[rows_w(0)], W[rows_w(1)], W[rows_w(2)]
        da = dot(dU_s[0, pl.ds(q0 + QUART, QUART)], wq, NT)
        p0 = pl.ds(t * QUART, QUART)
        back(
            da, n1q[p0].astype(f32), rq[p0], y_s[pl.ds(q0 + QUART, QUART)],
            pl.ds(2 * HALF + D + t * QUART, QUART), pl.ds(2 * HALF + t * QUART, QUART),
        )
        for b in range(4):
            at = pl.ds(pl.multiple_of(((f + b) % 4) * QUART, QUART), QUART)
            rows = pl.ds(pl.multiple_of(t * HALF + ((f + b) % 4) * QUART, QUART), QUART)
            da = dot(G_s[t, at], wk, NT) + dot(G_s[2 + t, at], wv, NT)
            extra = None
            if b == 0:
                da = da + dot(dU_s[0, pl.ds(q0, QUART)], wq, NT)
                extra = y_s[pl.ds(q0, QUART)]
            back(da, n1s[rows].astype(f32), rs[rows], extra, rows, rows)

    below(0)
    tick(3)
    tick(2)
    tick(0)
    tick(1)
    below(1)

    small_rows = pl.ds(0, 16)
    PK[0, small_rows] = sg[...]
    for k in range(2):
        PK[0, pl.ds(16 + k * PADF, PADF)] = eg[2 * k + 1 - c]

    def pk_copy(i):
        rows = pl.ds(0, 80 if i == 0 else 48)
        dev = core_id if i == 0 else x_id if i == 1 else row_id[i - 2]
        return remote(PK.at[i, rows], RK.at[i, rows], ps.at[i], pr.at[i], dev)

    def pk_step(i):
        pk_copy(i).wait_recv()
        if i == 0:
            PK[1, small_rows] = PK[0, small_rows] + RK[0, small_rows]
            own = [eg[2 * k + c] + RK[0, pl.ds(16 + k * PADF, PADF)] for k in range(2)]
            PK[1, pl.ds(16, PADF)] = jnp.where(x == 0, own[1], own[0])
            PK[1, pl.ds(48, PADF)] = jnp.where(x == 0, own[0], own[1])
            pk_copy(1).start()
        else:
            old = PK[1, pl.ds(48, PADF)] if i == 1 else PK[i, pl.ds(16, PADF)]
            a = PK[i, small_rows] + RK[i, small_rows]
            b = old + RK[i, pl.ds(16, PADF)]
            if i < n + 1:
                PK[i + 1, small_rows] = a
                PK[i + 1, pl.ds(16, PADF)] = b
                pk_copy(i + 1).start()
            else:
                SM[...] = a
                EM[...] = b

    pk_copy(0).start()
    gt1 = remote(GT.at[1 - c], GC, gs.at[0], gr.at[0], core_id)
    gt1.start()
    sup = pl.ds(0, 2 * HALF)
    que = pl.ds(2 * HALF, 512)

    def que_of(k):
        return pl.ds(pl.multiple_of(2 * HALF + k * 512, 512), 512)

    gt2 = remote(XS, XR, gs.at[1], gr.at[1], x_id)
    tick(0)
    tick(2)
    pk_step(0)
    gt1.wait_recv()
    XS[:, sup] = add(GT[c, 1 - x, :, sup], GC[1 - x, :, sup])
    XS[:, que_of(c)] = GT[c, 1 - x, :, que]
    XS[:, que_of(1 - c)] = GC[1 - x, :, que]
    gt2.start()
    tick(1)
    tick(3)
    next_pk = 1

    def select(m):
        for s in range(4):
            p = lax.rem(su[s], R)
            if m == 0:
                g = lax.rem(2 * lax.div(su[s], R) + 4, 6)
                value = AGB[g, p].astype(f32) * occ[s]
            else:
                g = 2 * lax.max(lax.div(su[s], R) - 1, 0) + 1
                value = AGB[g, p].astype(f32) * occ[4 + s] + AGL[p].astype(f32) * occ[8 + s]
            SEL[m, s] = value.astype(bf16)

    def fin(m, k):
        if k == 3:
            return pltpu.make_async_copy(SEL.at[m], FIN.at[m, f], osem.at[1 + m])
        src, at = (FIN.at[m, f ^ 2], f ^ 2) if k == 2 else (SEL.at[m], f)
        return remote(src, FIN.at[m, at], fs.at[m, k], fr.at[m, k], x_id if k == 1 else core_id)

    def send_fin(m):
        select(m)
        for k in (1, 0, 3):
            fin(m, k).start()

    sent = False
    while min(done) < last:
        for k in (0, 1, 2, 3):
            tick(k)
        if next_pk < n + 2:
            pk_step(next_pk)
            next_pk += 1
        if not sent and min(done[:3]) == last:
            send_fin(0)
            sent = True
    send_fin(1)
    for i in range(next_pk, n + 2):
        pk_step(i)
    gt2.wait_recv()
    GI[:, sup] = (
        GT[c, x, :, sup].astype(f32) + GC[x, :, sup].astype(f32) + XR[:, sup].astype(f32)
    ).astype(bf16)
    GI[:, que_of(f)] = GT[c, x, :, que]
    GI[:, que_of(f ^ 1)] = GC[x, :, que]
    for k in range(2):
        GI[:, que_of(2 * (1 - x) + k)] = XR[:, pl.ds(2 * HALF + k * 512, 512)]
    for m in range(2):
        fin(m, 1).wait_recv()
        fin(m, 2).start()
    for m in range(2):
        fin(m, 0).wait()
        fin(m, 1).wait_send()
        fin(m, 2).wait()
        fin(m, 3).wait()
    for k in range(4):
        core_copy(k).wait_send()
        x_copy(k).wait_send()
        for j in range(n):
            rs_copy(k, j).wait_send()
            ag_copy(k, j).wait_send()
    for i in range(n + 2):
        pk_copy(i).wait_send()
    gt1.wait_send()
    gt2.wait_send()
    ship_out.wait()


def main_call(R, su, occ, linv, small, W, O, h0, dY, ET, OT, q, kT, v, a1s, a1q, n1s, n1q, rs, rq, XT):
    BH = 12 * D // (3 * R) // 2
    n = R.bit_length() - 1
    sd = jax.ShapeDtypeStruct
    V = pltpu.VMEM
    dma = pltpu.SemaphoreType.DMA
    blk = (R, BH, 128)
    like = lambda a: V(a.shape, a.dtype)
    return pl.pallas_call(
        functools.partial(main_kernel, R),
        out_shape=(sd((1024, D), bf16), sd((2, 4, 4, BH, 128), bf16), sd((16, D), f32), sd((PADF, D), f32), sd((PADF, 4096), bf16)),
        in_specs=[smem(), smem(), vmem(), vmem()] + [anyspace()] * 16,
        out_specs=(anyspace(), anyspace(), vmem(), vmem(), vmem()),
        scratch_shapes=[
            like(W), like(O), like(h0), like(dY), V((4, HALF, 512), bf16), like(OT), like(q), like(kT), like(v),
            like(a1s), like(a1q), like(n1s), like(n1q), like(rs), like(rq), like(XT),
            V((1024, D), bf16), V((4, 1024, 512), bf16), V((4, 1024, 512), bf16), V((8, 512), f32), V((16, D), f32),
            V((4, PADF, D), f32), V((2, 2, PADF, 2560), bf16),
            V((2, 2, 6) + blk, bf16), V((2, 6) + blk, bf16), V((6,) + blk, bf16), V((6,) + blk, bf16), V((5,) + blk, bf16), V(blk, bf16),
            V((2, 4, BH, 128), bf16), V((n + 2, 80, D), f32), V((n + 2, 80, D), f32),
            V((2, PADF, 2560), bf16), V((PADF, 3072), bf16), V((PADF, 3072), bf16),
            dma((26,)), dma((4,)), dma((3,)), dma((4, 2 + 2 * n)), dma((4, 2 + 2 * n)), dma((2, 3)), dma((2, 3)),
            dma((n + 2,)), dma((n + 2,)), dma((2,)), dma((2,)),
        ],
        compiler_params=pltpu.CompilerParams(collective_id=1, has_side_effects=True, vmem_limit_bytes=VMEM_BYTES),
        name="main",
    )(su, occ, linv, small, W, O, h0, dY, ET, OT, q, kT, v, a1s, a1q, n1s, n1q, rs, rq, XT)


def adamw(weight, grad, first, second, rate):
    first_new = BETA_FIRST * first + (1.0 - BETA_FIRST) * grad
    second_new = BETA_SECOND * second + (1.0 - BETA_SECOND) * grad * grad
    first_hat = first_new / (1.0 - BETA_FIRST**STEP)
    second_hat = second_new / (1.0 - BETA_SECOND**STEP)
    weight_new = weight - rate * (first_hat / (jnp.sqrt(second_hat) + ADAM_EPS) + DECAY * weight)
    return (first_new, second_new, weight_new)


def update_kernel(
    occ, tmap, FIN, w, m, v, SM, sw, sm, sv, EM, ew, em, ev, GI, masks, lo,
    g_o, m_o, v_o, w_o, wc_o, eg_o, em_o, ev_o, ew_o, ec_o, sg_o, sm_o, sv_o, sw_o, gi_o, lo_o,
):
    s = pl.program_id(0)
    keep = occ[s]
    BH = FIN.shape[3]
    for f in range(4):
        rows = pl.ds((f // 2) * BH, BH)
        for k in range(2):
            cols = pl.ds(k * 256 + (f % 2) * 128, 128)
            g = FIN[k, f, 0].astype(f32)
            a, b, d = adamw(w[0, rows, cols], g, m[0, rows, cols], v[0, rows, cols], RATE_MATRIX)
            g_o[0, rows, cols] = g * keep
            m_o[0, rows, cols] = a * keep
            v_o[0, rows, cols] = b * keep
            d = d * keep
            w_o[0, rows, cols] = d
            wc_o[0, rows, cols] = d.astype(bf16)

    @pl.when(s == 0)
    def _():
        g = SM[0:10]
        a, b, d = adamw(sw[...], g, sm[...], sv[...], RATE_SMALL)
        sg_o[...] = g
        sm_o[...] = a
        sv_o[...] = b
        sw_o[...] = d
        nf = ew.shape[0]
        g = EM[pl.ds(0, nf)]
        a, b, d = adamw(ew[...], g, em[...], ev[...], RATE_EMBED)
        eg_o[...] = g
        em_o[...] = a
        ev_o[...] = b
        ew_o[...] = d
        ec_o[...] = d.astype(bf16)

    nf = gi_o.shape[1]
    t = s // 2
    keep_in = mask_column(masks, tmap[t])

    @pl.when(s % 2 == 0)
    def _():
        cols = pl.ds(pl.multiple_of(t * HALF, HALF), HALF)
        gi_o[t, :, 0, :] = (GI[pl.ds(0, nf), cols].astype(f32) * keep_in).astype(bf16)

    @pl.when(s % 2 == 1)
    def _():
        for k in range(4):
            cols = pl.ds(pl.multiple_of(2 * HALF + k * 512 + t * QUART, QUART), QUART)
            gi_o[t, :, 1, pl.ds(k * QUART, QUART)] = (GI[pl.ds(0, nf), cols].astype(f32) * keep_in).astype(bf16)

    lo_o[...] = lo[...]


def update_call(occ, tmap, FIN, w, m, v, SM, sw, sm, sv, EM, ew, em, ev, GI, masks, lo):
    S, BR, W = w.shape
    nf = ew.shape[0]
    sd = jax.ShapeDtypeStruct
    blk = pl.BlockSpec((1, BR, W), lambda s: (s, 0, 0))
    whole = lambda a: pl.BlockSpec(a.shape, lambda s: (0,) * len(a.shape))
    ins = [smem(), smem(), pl.BlockSpec((2, 4, 1, BR // 2, 128), lambda s: (0, 0, s, 0, 0)), blk, blk, blk]
    ins += [whole(a) for a in (SM, sw, sm, sv, EM, ew, em, ev, GI, masks)] + [pl.BlockSpec((1024 // S, D), lambda s: (s, 0))]
    big = sd((S, BR, W), f32)
    small = sd((10, D), f32)
    e = sd((nf, D), f32)
    outs = [big, big, big, big, sd((S, BR, W), bf16), e, e, e, e, sd((nf, D), bf16), small, small, small, small, sd((2, nf, 2, HALF), bf16), sd(lo.shape, lo.dtype)]
    specs = [blk] * 5 + [whole(a) for a in outs[5:14]] + [whole(outs[14]), pl.BlockSpec((1024 // S, D), lambda s: (s, 0))]
    return pl.pallas_call(
        update_kernel, out_shape=tuple(outs), grid=(S,), in_specs=ins, out_specs=tuple(specs),
        compiler_params=pltpu.CompilerParams(vmem_limit_bytes=VMEM_BYTES), name="update",
    )(occ, tmap, FIN, w, m, v, SM, sw, sm, sv, EM, ew, em, ev, GI, masks, lo)


def body(
    features, feature_masks, table_map, owners, out_grad, weight_slots, moment1_slots, moment2_slots,
    emb_weight, emb_moment1, emb_moment2, small_weight, small_moment1, small_moment2,
):
    unit_count = owners.shape[0]
    capacity, block_rows, width = weight_slots.shape
    R = lax.axis_size("rows")
    bits = R.bit_length() - 1
    my_row = lax.axis_index("rows")
    units = jnp.arange(unit_count, dtype=jnp.int32)
    same_owner = owners[:, None] == owners[None, :]
    owner_rank = jnp.sum((same_owner & (units[None, :] < units[:, None])).astype(jnp.int32), axis=1)
    distance = owners ^ my_row
    place = jnp.zeros_like(distance)
    for bit in range(bits):
        place = place | (((distance >> bit) & 1) << (bits - 1 - bit))
    pos = place * capacity + owner_rank
    slot_iota = jnp.arange(capacity, dtype=jnp.int32)
    hit = (owners[None, :] == my_row) & (owner_rank[None, :] == slot_iota[:, None])
    slot_unit = jnp.sum(jnp.where(hit, units[None, :], 0), axis=1)
    occupied = jnp.sum(hit.astype(f32), axis=1)

    masks = feature_masks.T
    late = occupied * (slot_unit < R).astype(f32)
    kinds = jnp.concatenate([occupied, occupied - late, late])
    G, XT, h0o, a1s, a1q, n1s, n1q, rs, rq = gather_call(
        R, weight_slots, features.transpose(0, 3, 1, 2), masks, table_map, emb_weight, small_weight
    )
    G = G.reshape(R * capacity, block_rows, width)
    dY = out_grad.reshape(1024, width)
    W, linv, q, kT, v, ET, OT, O = forward_call(pos, G, a1s, a1q)
    out, FIN, SM, EM, GI = main_call(
        R, slot_unit, kinds, linv, small_weight, W, O, h0o, dY, ET, OT, q, kT, v, a1s, a1q, n1s, n1q, rs, rq, XT
    )
    (
        g_slots, m_slots, v_slots, w_slots, w_copy, e_grad, e_m, e_v, e_w, e_copy, s_grad, s_m, s_v, s_w, grad_inputs, out,
    ) = update_call(
        kinds, table_map, FIN, weight_slots, moment1_slots, moment2_slots, SM, small_weight, small_moment1,
        small_moment2, EM, emb_weight, emb_moment1, emb_moment2, GI, masks, out,
    )
    grad_inputs = grad_inputs.transpose(0, 2, 3, 1)
    return (
        out.reshape(out_grad.shape), grad_inputs, g_slots, m_slots, v_slots, w_slots, w_copy,
        e_grad, e_m, e_v, e_w, e_copy, s_grad, s_m, s_v, s_w,
    )


def solution(mesh):
    rows3 = P("rows", None, None)
    feat2 = P("feat", None)
    in_specs = (
        P("rows", None, None, "feat"), P(None, "feat"), P("rows"), P(), P("rows", None, "feat", None),
        rows3, rows3, rows3, feat2, feat2, feat2, P(), P(), P(),
    )
    out_specs = (
        P("rows", None, "feat", None), P("rows", None, None, "feat"), rows3, rows3, rows3, rows3, rows3,
        feat2, feat2, feat2, feat2, feat2, P(), P(), P(), P(),
    )
    return jax.shard_map(body, mesh=mesh, in_specs=in_specs, out_specs=out_specs, check_vma=False)
```

time: 215 us -> 193 us (0.90)
  Pallas kernels: 205 us -> 186 us
  local copies, waits for them, and re-layouts: 4.38 us -> 1.38 us
    pallas_call x2, Pallas kernels: 136 us -> 117 us  [the longest x1 99.3 us: main_call(): pl.pallas_call(functools.partial(main_kernel, R), out_shape=(sd((1024, D)...]
    unnamed x2 -> x3, local copies, waits for them, and re-layouts: 4.38 us -> 1.38 us
where the time goes in v3:
time: 193 us; the launch traced here: 192 us
  Pallas kernels  186 us (96%)
  other arithmetic  3.61 us (2%)
    pallas_call x1, Pallas kernels, main_call(): pl.pallas_call(functools.partial(main_kernel, R), out_shape=(sd((1024, D)...  99.3 us
    pallas_call x1, Pallas kernels, gather_call(): pl.pallas_call(functools.partial(gather_kernel, R), out_shape=(sd((R, S,...  59.5 us
    pallas_call x1, Pallas kernels, forward_call(): pl.pallas_call(functools.partial(forward_kernel, BR), out_shape=(sd((12 *...  17.8 us
    pallas_call x1, Pallas kernels, update_call(): pl.pallas_call(update_kernel, out_shape=tuple(outs), grid=(S,), in_specs=...  9.28 us

profile of v3, /device:TPU:0, one launch (start us, length us, event | category | flops | bytes accessed | tf_op | source)
XLA Modules:
  0.0 191.7 jit_solution(147575359298977108)
XLA Ops:
  0.6 0.9 convert_reduce_fusion
  1.6 0.7 broadcast_compare_fusion
  2.2 1.2 multiply_add_fusion.pos
  3.4 0.1 select_reduce_fusion.su
  3.5 0.0 copy-start
  3.5 0.1 convert_reduce_fusion.1
  3.6 0.6 pad_maximum_fusion.occ
  4.3 1.4 copy.31
  5.6 59.5 %gather_weights.1 = (bf16[8,4,256,512]{3,2,1,0:T(8,128)(2,1)}, bf16[128,3072]{1,0:T(8,128)(2,1)}, f32[1024,512]{1,0:T(8,128)}, bf16[2048,512]{1,0:T(8,128)(2,1)}...) custom-call(f32[4,256,512]{2,1,0:T(8,128)} %w.1, ...), custom_call_target="tpu_custom_call" | custom-call | tf_op jit(solution)/shard_map/gather_weights/pallas_call | solution.py:245
  65.1 17.8 %forward.1 = (bf16[6144,512]{1,0:T(8,128)(2,1)}, f32[8,512]{1,0:T(8,128)}, bf16[1024,512]{1,0:T(8,128)(2,1)}, bf16[512,2048]{1,0:T(8,128)(2,1)}, bf16[2048,512]{...) custom-call(s32[24]{0:T(128)} %multiply_add_fusion.pos, ...), custom_call_target="tpu_custom_call" | custom-call | tf_op jit(solution)/shard_map/forward/pallas_call | solution.py:362
  82.9 0.0 copy-done
  82.9 99.3 %main.1 = (bf16[1024,512]{1,0:T(8,128)(2,1)}, bf16[2,4,4,128,128]{4,3,2,1,0:T(8,128)(2,1)}, f32[16,512]{1,0:T(8,128)}, f32[32,512]{1,0:T(8,128)}, bf16[32,4096]{1,0:T(8,128)(2,1)}) custom-call(s32[4]{0:T(128)} %copy-done, f32[12]{0:T(128)} %pad_maximum_fusion.occ, f32[8,512]{1,0:T(8,128)} %get-tuple-element.57.linv, f32[10,512]{1,0:T(8,128)} %sw.1, ...), custom_call_target="tpu_custom_call" | custom-call | tf_op jit(solution)/shard_map/main/pallas_call | solution.py:835
  182.2 9.3 %update.1 = (f32[4,256,512]{2,1,0:T(8,128)}, f32[4,256,512]{2,1,0:T(8,128)}, f32[4,256,512]{2,1,0:T(8,128)}, f32[4,256,512]{2,1,0:T(8,128)}, bf16[4,256,512]{2,1...) custom-call(f32[12]{0:T(128)} %pad_maximum_fusion.occ, ...), custom_call_target="tpu_custom_call" | custom-call | tf_op jit(solution)/shard_map/update/pallas_call | solution.py:933
  (1 shorter events, 0.0 us)
Async XLA Ops:
  3.5 79.4 %copy-start = (s32[4]{0:T(128)}, s32[4]{0:T(128)S(1)}, u32[]{:S(2)}) copy-start(s32[4]{0:T(128)S(1)} %select_reduce_fusion.su) | copy-start | bytes 52
